TPU v7x, 256 devices: a whole 4x4x8 slice. The times are simulated.
256 devices in a mesh: row: 16 (over z, core), col: 16 (over x, y).
Axes of the slice: x: 4, y: 4, z: 8, core: 2. Of those that a mesh axis runs over, the one named last changes fastest.
Arguments:
- left_panel: bfloat16 [2, 16384, 1024], P(None, 'row', 'col'), may hold values from -0.125 to 0.125
- right_panel: bfloat16 [2, 1024, 16384], P(None, 'row', 'col'), may hold values from -6 to 6
Outputs:
- multiples: float32 [2, 16384, 16384], P(None, 'row', 'col')
All inputs are finite; a program needn't handle non-finite values.
Results may differ from a plain program's by a relative error of at most 0.0003.
Values may be sent and summed in bfloat16 or wider, within the bound.
No kernel may reach another device: no remote copies, remote signals or barrier semaphores. Data moves between devices by JAX's collectives and lax.ppermute only.
A program may use at most 64 MiB of HBM per device.

v0:
```python
import jax
import jax.numpy as jnp
from jax import lax
from jax.sharding import PartitionSpec as P


def complex_block(left_part, right_part):
    left_real, left_imag = (left_part[0], left_part[1])
    right_real, right_imag = (right_part[0], right_part[1])
    real_part = jnp.dot(left_real, right_real, preferred_element_type=jnp.float32) - jnp.dot(
        left_imag, right_imag, preferred_element_type=jnp.float32
    )
    imag_part = jnp.dot(left_real, right_imag, preferred_element_type=jnp.float32) + jnp.dot(
        left_imag, right_real, preferred_element_type=jnp.float32
    )
    return jnp.stack([real_part, imag_part])


def local(left_panel, right_panel):
    right_all = lax.all_gather(right_panel, "row", axis=1, tiled=True)
    left_all = lax.all_gather(left_panel, "col", axis=2, tiled=True)
    multiples = complex_block(left_all, right_all)
    return multiples


def solution(mesh):
    placed = (P(None, "row", "col"), P(None, "row", "col"))
    return jax.shard_map(
        local, mesh=mesh, in_specs=placed, out_specs=P(None, "row", "col"), check_vma=False
    )
```

profile of v0, /device:TPU:1, one launch (start us, length us, event | category | flops | bytes accessed | tf_op | source)
XLA Modules:
  0.0 137.9 jit_solution(7791604669040885092)
XLA Ops:
  6.5 0.0 all-gather.3.cloned.1.call-start
  6.5 0.7 all-gather.3.cloned.1.call-update
  7.3 0.0 all-gather.5.cloned.1.call-start
  7.3 0.7 all-gather.5.cloned.1.call-update
  8.0 62.3 %all-gather.3.cloned.1.call-done = bf16[2,1024,1024]{1,2,0:T(8,128)(2,1)} async-done(((bf16[2,1024,64]{1,2,0:T(8,128)(2,1)}), bf16[2,1024,1024]{1,2,0:T(8,128)(2,1)}) %all-gather.3.cloned.1.call-update) | async-done | bytes 4194320 | tf_op jit(solution)/shard_map/all_gather | solution.py:21
  70.3 44.2 %all-gather.5.cloned.1.call-done = bf16[2,1024,1024]{2,1,0:T(8,128)(2,1)} async-done(((bf16[2,64,1024]{2,1,0:T(8,128)(2,1)}), bf16[2,1024,1024]{2,1,0:T(8,128)(2,1)}) %all-gather.5.cloned.1.call-update) | async-done | bytes 4194320 | tf_op jit(solution)/shard_map/all_gather | solution.py:20
  114.5 0.0 copy-start
  114.5 0.0 copy-start.1
  114.5 4.8 %fusion = f32[1024,1024]{1,0:T(8,128)S(1)} fusion(bf16[2,1024,1024]{1,2,0:T(8,128)(2,1)} %all-gather.3.cloned.1.call-done, bf16[2,1024,1024]{2,1,0:T(8,128)(2,1)} %all-gather.5.cloned.1.call-done), kind=kOutput, calls=%fused_computation.7 | convolution fusion | flops 2147483648 | bytes 8388608 | tf_op jit(solution)/shard_map/dot_general | solution.py:13
  119.2 0.0 copy-done
  119.2 0.0 copy-done.1
  119.2 2.4 %fusion.1 = f32[1024,1024]{1,0:T(8,128)S(1)} fusion(bf16[2,1024,1024]{1,2,0:T(8,128)(2,1)S(1)} %copy-done, bf16[2,1024,1024]{2,1,0:T(8,128)(2,1)S(1)} %copy-done.1), kind=kOutput, calls=%fused_computation.8 | convolution fusion | flops 2147483648 | bytes 8388608 | tf_op jit(solution)/shard_map/dot_general | solution.py:10
  121.6 2.6 %add_bitcast_fusion = f32[1,1024,1024]{2,1,0:T(8,128)S(1)} fusion(f32[1024,1024]{1,0:T(8,128)S(1)} %fusion, bf16[2,1024,1024]{2,1,0:T(8,128)(2,1)S(1)} %copy-done.1, bf16[2,1024,1024]{1,2,0:T(8,128)(2,1)S(1)} %copy-done), kind=kOutput, calls=%fused_computation.1 | convolution fusion | flops 2148532224 | bytes 12582912 | tf_op jit(solution)/shard_map/dot_general | solution.py:13
  124.2 2.6 %subtract_bitcast_fusion = f32[1,1024,1024]{2,1,0:T(8,128)S(1)} fusion(f32[1024,1024]{1,0:T(8,128)S(1)} %fusion.1, bf16[2,1024,1024]{1,2,0:T(8,128)(2,1)S(1)} %copy-done, bf16[2,1024,1024]{2,1,0:T(8,128)(2,1)S(1)} %copy-done.1), kind=kOutput, calls=%fused_computation.2 | convolution fusion | flops 2148532224 | bytes 12582912 | tf_op jit(solution)/shard_map/dot_general | solution.py:10
  126.8 4.2 %pad_maximum_fusion = f32[2,1024,1024]{2,1,0:T(8,128)} fusion(f32[1,1024,1024]{2,1,0:T(8,128)S(1)} %add_bitcast_fusion, f32[1,1024,1024]{2,1,0:T(8,128)S(1)} %subtract_bitcast_fusion), kind=kLoop, calls=%fused_computation | loop fusion | flops 2097152 | bytes 16777216 | tf_op jit(solution)/shard_map/stack | solution.py:16
Async XLA Ops:
  6.5 63.8 %all-gather.3.cloned.1.call-start = ((), (), s32[]{:S(2)}) async-start(), calls=%async_computation | async-start | bytes 4456448 | tf_op jit(solution)/shard_map/all_gather | solution.py:21
  7.3 107.2 %all-gather.5.cloned.1.call-start = ((), (), s32[]{:S(2)}) async-start(), calls=%async_computation.1 | async-start | bytes 4456448 | tf_op jit(solution)/shard_map/all_gather | solution.py:20
  114.5 4.8 %copy-start = (bf16[2,1024,1024]{1,2,0:T(8,128)(2,1)S(1)}, bf16[2,1024,1024]{1,2,0:T(8,128)(2,1)}, u32[]{:S(2)}) copy-start(bf16[2,1024,1024]{1,2,0:T(8,128)(2,1)} %all-gather.3.cloned.1.call-done) | copy-start | bytes 12582916
  114.5 4.8 %copy-start.1 = (bf16[2,1024,1024]{2,1,0:T(8,128)(2,1)S(1)}, bf16[2,1024,1024]{2,1,0:T(8,128)(2,1)}, u32[]{:S(2)}) copy-start(bf16[2,1024,1024]{2,1,0:T(8,128)(2,1)} %all-gather.5.cloned.1.call-done) | copy-start | bytes 12582916
Sparse Core Ops, SparseCore 0:
  9.8 60.4 all-gather.2
  72.1 42.2 all-gather.4
where the time goes:
time: 138 us
  waiting for transfers between devices  108 us (78%)
  between operations  13.4 us (10%)
  matrix products  12.3 us (9%)
  other arithmetic  4.24 us (3%)
    all_gather x1, waiting for transfers between devices, local(): left_all = lax.all_gather(left_panel, 'col', axis=2, tiled=True)  62.3 us
    all_gather x1, waiting for transfers between devices, local(): right_all = lax.all_gather(right_panel, 'row', axis=1, tiled=True)  44.2 us
    dot_general x1, matrix products, complex_block(): jnp.dot(left_real, right_imag, preferred_element_type=jnp.float32)  4.75 us
    another operation x1, other arithmetic, complex_block(): return jnp.stack([real_part, imag_part])  4.24 us
  transfers between devices with their start and end apart: 2, of which 2 were waited for; matrix products, arithmetic and copies ran while one was open for 0% of the time, Pallas kernels for 0%

commit v1 on v0

v1 whole, which is shorter than its diff:
```python
import jax
import jax.numpy as jnp
from jax import lax
from jax.experimental import pallas as pl
from jax.experimental.pallas import tpu as pltpu
from jax.sharding import PartitionSpec as P

AXES = ("row", "col")
RING = (0, -1, 1, 2)


def permute(value, target):
    pairs = []
    for z in range(8):
        for core in range(2):
            for x in range(4):
                for y in range(4):
                    to_z, to_core, to_x, to_y = target(z, core, x, y)
                    pairs.append(
                        (
                            (z * 2 + core) * 16 + x * 4 + y,
                            (to_z % 8 * 2 + to_core) * 16 + to_x % 4 * 4 + to_y % 4,
                        )
                    )
    return lax.ppermute(value, AXES, pairs)


def first_axis(step):
    return lambda z, c, x, y: (z, c, x + step, y) if c == 0 else (z, c, x, y + step)


def second_axis(step):
    return lambda z, c, x, y: (z, c, x, y + step) if c == 0 else (z, c, x + step, y)


def along_z(step):
    return lambda z, c, x, y: (z + step, c, x, y) if c == 0 else (z - step, c, x, y)


def other_core(z, c, x, y):
    return (z, 1 - c, x, y)


def product(left, right, m, rows):
    depth = left.shape[0] * 64
    pick = lambda plane: left[:, plane, :, pl.ds(m, rows)].reshape(depth, rows)
    take = lambda plane: right[:, plane].reshape(depth, 1024)
    dot = lambda a, b: lax.dot_general(
        a, b, (((0,), (0,)), ((), ())), preferred_element_type=jnp.float32
    )
    l0, l1, r0, r1 = pick(0), pick(1), take(0), take(1)
    return dot(l0, r0) - dot(l1, r1), dot(l0, r1) + dot(l1, r0)


def early_kernel(n_right, places, *refs):
    right_parts, left_parts = refs[:n_right], refs[n_right : n_right + 3]
    acc, last, left, right, sems = refs[n_right + 3 :]
    copies = []
    slot = 0
    for part in right_parts:
        for b in range(part.shape[0]):
            copies.append(
                pltpu.make_async_copy(part.at[b], right.at[places[slot]], sems.at[slot])
            )
            slot += 1
    for g, part in enumerate(left_parts):
        copies.append(
            pltpu.make_async_copy(part, left.at[pl.ds(4 * g, 4)], sems.at[slot + g])
        )
    for copy in copies:
        copy.start()
    for copy in copies:
        copy.wait()

    @pl.loop(0, 4)
    def _(t):
        m = pl.multiple_of(t * 256, 256)
        real, imag = product(left, right.at[pl.ds(0, 12)], m, 256)
        acc[0, pl.ds(m, 256)] = real
        acc[1, pl.ds(m, 256)] = imag

    last[...] = right[12:16]


def early(places, right_parts, left_parts):
    n = len(right_parts)
    anywhere = pl.BlockSpec(memory_space=pl.ANY)
    return pl.pallas_call(
        lambda *refs: early_kernel(n, *refs),
        out_shape=[
            pltpu.VMEM((2, 1024, 1024), jnp.float32),
            pltpu.VMEM((4, 2, 64, 1024), jnp.bfloat16),
        ],
        in_specs=[pl.BlockSpec(memory_space=pltpu.SMEM)] + [anywhere] * (n + 3),
        out_specs=[pl.BlockSpec(memory_space=pltpu.VMEM)] * 2,
        scratch_shapes=[
            pltpu.VMEM((12, 2, 64, 1024), jnp.bfloat16),
            pltpu.VMEM((16, 2, 64, 1024), jnp.bfloat16),
            pltpu.SemaphoreType.DMA((19,)),
        ],
        compiler_params=pltpu.CompilerParams(vmem_limit_bytes=40 * 2**20),
        cost_estimate=pl.CostEstimate(
            flops=6 * 2**30, bytes_accessed=8 * 2**20, transcendentals=0
        ),
    )(places, *right_parts, *left_parts)


def late_kernel(acc, right, left, out):
    m = pl.multiple_of(pl.program_id(0) * 128, 128)
    real, imag = product(left, right, m, 128)
    out[0] = acc[0, pl.ds(m, 128)] + real
    out[1] = acc[1, pl.ds(m, 128)] + imag


def late(acc, right, left):
    whole = pl.BlockSpec(memory_space=pltpu.VMEM)
    acc = pltpu.with_memory_space_constraint(acc, pltpu.VMEM)
    right = pltpu.with_memory_space_constraint(right, pltpu.VMEM)
    return pl.pallas_call(
        late_kernel,
        grid=(8,),
        out_shape=jax.ShapeDtypeStruct((2, 1024, 1024), jnp.float32),
        in_specs=[whole, whole, whole],
        out_specs=pl.BlockSpec((2, 128, 1024), lambda i: (0, i, 0)),
        compiler_params=pltpu.CompilerParams(vmem_limit_bytes=40 * 2**20),
        cost_estimate=pl.CostEstimate(
            flops=2 * 2**30, bytes_accessed=9 * 2**20, transcendentals=0
        ),
    )(acc, right, left)


def right_places():
    row, col = lax.axis_index("row"), lax.axis_index("col")
    z, core, x, y = row // 2, row % 2, col // 4, col % 4
    sign = 1 - 2 * core
    owners = []
    for far in range(4):
        for c in (core, 1 - core):
            owners.append((z - sign * far, c))
    owners.append((z - sign * 4, core))
    for far in range(1, 4):
        for c in (1 - core, core):
            owners.append((z + sign * far, c))
    owners.append((z - sign * 4, 1 - core))
    trace = jnp.stack([zz % 8 * 2 + c for zz, c in owners])
    dx, dy = (trace // 4 - x) % 4, (trace % 4 - y) % 4
    member = jnp.where(core == 0, dx, dy)
    group = jnp.where(core == 0, dy, dx)
    order = lambda d: jnp.where(d == 3, 1, jnp.where(d == 1, 2, jnp.where(d == 2, 3, 0)))
    return (order(group) * 4 + order(member)).astype(jnp.int32)


def local(left_panel, right_panel):
    own = jnp.swapaxes(left_panel, 1, 2)
    ring = jnp.stack([own] + [permute(own, first_axis(d)) for d in (1, -1, 2)])
    groups = [ring] + [permute(ring, second_axis(d)) for d in (1, -1, 2)]

    pair = jnp.stack([right_panel, permute(right_panel, other_core)])
    rights = [pair]
    for _ in range(3):
        rights.append(permute(rights[-1], along_z(1)))
    rights.append(permute(rights[-1][:1], along_z(1)))
    rights += [permute(part, other_core) for part in rights[1:]]

    acc, last = early(right_places(), rights, groups[:3])
    return late(acc, last, groups[3])


def solution(mesh):
    placed = (P(None, "row", "col"), P(None, "row", "col"))
    return jax.shard_map(
        local, mesh=mesh, in_specs=placed, out_specs=P(None, "row", "col"), check_vma=False
    )
```

time: 138 us -> 67.4 us (0.49)
  waiting for transfers between devices: 108 us -> 13 us
  starting transfers between devices: 0.04 us -> 30.2 us
  Pallas kernels: 0 us -> 17.1 us
  between operations: 13.4 us -> 0.07 us
  matrix products: 12.3 us -> 0 us
  local copies, waits for them, and re-layouts: 0.01 us -> 3.62 us
    all_gather x2 -> x0, waiting for transfers between devices: 106 us -> none  [the longest x1 62.3 us: local(): left_all = lax.all_gather(left_panel, 'col', axis=2, tiled=True)]
    ppermute x0 -> x15, starting transfers between devices: none -> 30.2 us  [permute(): return lax.ppermute(value, AXES, pairs)]
    pallas_call x0 -> x2, Pallas kernels: none -> 17.1 us  [the longest x1 10.6 us: early(): pl.pallas_call(lambda *refs: early_kernel(n, *refs), out_shape=[pltpu.VME...]
    ppermute x0 -> x15, waiting for transfers between devices: none -> 13 us  [permute(): return lax.ppermute(value, AXES, pairs)]
    dot_general x4 -> x0, matrix products: 12.3 us -> none  [the longest x1 4.75 us: complex_block(): jnp.dot(left_real, right_imag, preferred_element_type=jnp.float32)]
    unnamed x4 -> x10, local copies, waits for them, and re-layouts: 0.01 us -> 3.51 us
    unnamed x2 -> x0, waiting for transfers between devices: 1.41 us -> none
    another operation x1 -> x2, other arithmetic: 4.24 us -> 3.05 us  [the longest x1 2.05 us: local(): ring = jnp.stack([own] + [permute(own, first_axis(d)) for d in (1, -1, 2)])]
  transfers between devices with their start and end apart: 2 -> 15, of which waited for: 2 -> 5; matrix products, arithmetic and copies ran while one was open for 0% -> 3% of each run, Pallas kernels for 0% -> 16%
where the time goes in v1:
time: 67.4 us; the launch traced here: 67.2 us
  starting transfers between devices  30.2 us (45%)
  Pallas kernels  17.1 us (25%)
  waiting for transfers between devices  13 us (19%)
  local copies, waits for them, and re-layouts  3.62 us (5%)
  other arithmetic  3.08 us (5%)
    ppermute x15, starting transfers between devices, permute(): return lax.ppermute(value, AXES, pairs)  30.2 us
    ppermute x15, waiting for transfers between devices, permute(): return lax.ppermute(value, AXES, pairs)  13 us
    pallas_call x1, Pallas kernels, early(): pl.pallas_call(lambda *refs: early_kernel(n, *refs), out_shape=[pltpu.VME...  10.6 us
    pallas_call x1, Pallas kernels, late(): pl.pallas_call(late_kernel, grid=(8,), out_shape=jax.ShapeDtypeStruct((2,...  6.51 us
    unnamed x10, local copies, waits for them, and re-layouts  3.51 us
    another operation x1, other arithmetic, local(): ring = jnp.stack([own] + [permute(own, first_axis(d)) for d in (1, -1, 2)])  2.05 us
  transfers between devices with their start and end apart: 15, of which 5 were waited for; matrix products, arithmetic and copies ran while one was open for 3% of the time, Pallas kernels for 16%

profile of v1, /device:TPU:1, one launch (start us, length us, event | category | flops | bytes accessed | tf_op | source)
XLA Modules:
  0.0 67.2 jit_solution(11465565686097143564)
XLA Ops:
  0.0 3.2 %collective-permute-start = (bf16[2,64,1024]{2,1,0:T(8,128)(2,1)}, bf16[2,64,1024]{2,1,0:T(8,128)(2,1)S(1)}, u32[]{:S(2)}, u32[]{:S(2)}) collective-permute-start(bf16[2,64,1024]{2,1,0:T(8,128)(2,1)} %param.3), channel_id=1, source_target_pairs={{0,16},{1,17},{2,18},{3,19},{4,20},{5,21},{6,22},{7,23},{8,24},{9,... | collective-permute-start | bytes 786440 | tf_op jit(solution)/shard_map/ppermute | solution.py:25
  3.2 1.4 %collective-permute-done = bf16[2,64,1024]{2,1,0:T(8,128)(2,1)S(1)} collective-permute-done((bf16[2,64,1024]{2,1,0:T(8,128)(2,1)}, bf16[2,64,1024]{2,1,0:T(8,128)(2,1)S(1)}, u32[]{:S(2)}, u32[]{:S(2)}) %collective-permute-start) | collective-permute-done | bytes 262176 | tf_op jit(solution)/shard_map/ppermute | solution.py:25
  4.6 1.0 %pad_maximum_fusion.1.refs_1_ = bf16[2,2,64,1024]{3,2,1,0:T(8,128)(2,1)S(1)} fusion(bf16[1,2,64,1024]{3,2,1,0:T(8,128)(2,1)S(1)} %bitcast.25, bf16[1,2,64,1024]{3,2,1,0:T(8,128)(2,1)} %bitcast.24), kind=kLoop, calls=%fused_computation.1 | loop fusion | flops 262144 | bytes 1048576 | tf_op jit(solution)/shard_map/stack | solution.py:158
  5.6 3.9 %collective-permute-start.1 = (bf16[2,2,64,1024]{3,2,1,0:T(8,128)(2,1)S(1)}, bf16[2,2,64,1024]{3,2,1,0:T(8,128)(2,1)S(1)}, u32[]{:S(2)}, u32[]{:S(2)}) collective-permute-start(bf16[2,2,64,1024]{3,2,1,0:T(8,128)(2,1)S(1)} %pad_maximum_fusion.1.refs_1_), channel_id=1, source_target_pairs={{0,32},{1,33},{2,34},{3,35},{4,36},{5,37},{6,38},{7,39},{8,40},{9,... | collective-permute-start | bytes 1572872 | tf_op jit(solution)/shard_map/ppermute | solution.py:25
  9.5 2.7 %collective-permute-start.10 = (bf16[2,64,1024]{2,1,0:T(8,128)(2,1)}, bf16[2,64,1024]{2,1,0:T(8,128)(2,1)S(1)}, u32[]{:S(2)}, u32[]{:S(2)}) collective-permute-start(bf16[2,64,1024]{2,1,0:T(8,128)(2,1)} %bitcast.26), channel_id=1, source_target_pairs={{0,12},{1,13},{2,14},{3,15},{4,0},{5,1},{6,2},{7,3},{8,4},{9,5},{1... | collective-permute-start | bytes 786440 | tf_op jit(solution)/shard_map/ppermute | solution.py:25
  12.3 0.0 collective-permute-start.9
  12.3 1.6 %collective-permute-start.11 = (bf16[2,64,1024]{2,1,0:T(8,128)(2,1)}, bf16[2,64,1024]{2,1,0:T(8,128)(2,1)S(1)}, u32[]{:S(2)}, u32[]{:S(2)}) collective-permute-start(bf16[2,64,1024]{2,1,0:T(8,128)(2,1)} %bitcast.28), channel_id=1, source_target_pairs={{0,8},{1,9},{2,10},{3,11},{4,12},{5,13},{6,14},{7,15},{8,0},{9,1},... | collective-permute-start | bytes 786440 | tf_op jit(solution)/shard_map/ppermute | solution.py:25
  13.9 1.7 %collective-permute-done.1.refs_2_ = bf16[2,2,64,1024]{3,2,1,0:T(8,128)(2,1)S(1)} collective-permute-done((bf16[2,2,64,1024]{3,2,1,0:T(8,128)(2,1)S(1)}, bf16[2,2,64,1024]{3,2,1,0:T(8,128)(2,1)S(1)}, u32[]{:S(2)}, u32[]{:S(2)}) %collective-permute-start.1) | collective-permute-done | bytes 524320 | tf_op jit(solution)/shard_map/ppermute | solution.py:25
  15.7 3.4 %collective-permute-start.2 = (bf16[2,2,64,1024]{3,2,1,0:T(8,128)(2,1)S(1)}, bf16[2,2,64,1024]{3,2,1,0:T(8,128)(2,1)}, u32[]{:S(2)}, u32[]{:S(2)}) collective-permute-start(bf16[2,2,64,1024]{3,2,1,0:T(8,128)(2,1)S(1)} %collective-permute-done.1.refs_2_), channel_id=1, source_target_pairs={{0,32},{1,33},{2,34},{3,35},{4,36},{5,37},{6,38},{7,39},{8,40},{9,... | collective-permute-start | bytes 1572872 | tf_op jit(solution)/shard_map/ppermute | solution.py:25
  19.1 0.0 collective-permute-done.10
  19.1 3.0 %collective-permute-done.9 = bf16[2,64,1024]{2,1,0:T(8,128)(2,1)S(1)} collective-permute-done((bf16[2,64,1024]{2,1,0:T(8,128)(2,1)}, bf16[2,64,1024]{2,1,0:T(8,128)(2,1)S(1)}, u32[]{:S(2)}, u32[]{:S(2)}) %collective-permute-start.9) | collective-permute-done | bytes 262176 | tf_op jit(solution)/shard_map/ppermute | solution.py:25
  22.1 0.0 collective-permute-done.11
  22.1 2.1 %pad_maximum_fusion.refs_10_ = bf16[4,2,64,1024]{3,2,1,0:T(8,128)(2,1)} fusion(bf16[1,2,64,1024]{3,2,1,0:T(8,128)(2,1)S(1)} %bitcast.32, bf16[1,2,64,1024]{3,2,1,0:T(8,128)(2,1)S(1)} %bitcast.30, bf16[1,2,64,1024]{3,2,1,0:T(8,128)(2,1)S(1)} %bitcast.31, bf16[1,2,64,1024]{3,2,1,0:T(8,128)(2,1)} %bitcast.29), kind=kLoop, calls=%fused_computation | loop fusion | flops 1572864 | bytes 2097152 | tf_op jit(solution)/shard_map/stack | solution.py:155
  24.2 2.5 %collective-permute-start.13 = (bf16[4,2,64,1024]{3,2,1,0:T(8,128)(2,1)}, bf16[4,2,64,1024]{3,2,1,0:T(8,128)(2,1)S(1)}, u32[]{:S(2)}, u32[]{:S(2)}) collective-permute-start(bf16[4,2,64,1024]{3,2,1,0:T(8,128)(2,1)} %pad_maximum_fusion.refs_10_), channel_id=1, source_target_pairs={{0,3},{1,0},{2,1},{3,2},{4,7},{5,4},{6,5},{7,6},{8,11},{9,8},{10,9... | collective-permute-start | bytes 3145736 | tf_op jit(solution)/shard_map/ppermute | solution.py:25
  26.7 0.0 collective-permute-done.2.refs_3_
  26.7 1.8 %collective-permute-start.3 = (bf16[2,2,64,1024]{3,2,1,0:T(8,128)(2,1)}, bf16[2,2,64,1024]{3,2,1,0:T(8,128)(2,1)S(1)}, u32[]{:S(2)}, u32[]{:S(2)}) collective-permute-start(bf16[2,2,64,1024]{3,2,1,0:T(8,128)(2,1)} %collective-permute-done.2.refs_3_), channel_id=1, source_target_pairs={{0,32},{1,33},{2,34},{3,35},{4,36},{5,37},{6,38},{7,39},{8,40},{9,... | collective-permute-start | bytes 1572872 | tf_op jit(solution)/shard_map/ppermute | solution.py:25
  28.4 1.1 %collective-permute-start.12 = (bf16[4,2,64,1024]{3,2,1,0:T(8,128)(2,1)}, bf16[4,2,64,1024]{3,2,1,0:T(8,128)(2,1)}, u32[]{:S(2)}, u32[]{:S(2)}) collective-permute-start(bf16[4,2,64,1024]{3,2,1,0:T(8,128)(2,1)} %pad_maximum_fusion.refs_10_), channel_id=1, source_target_pairs={{0,1},{1,2},{2,3},{3,0},{4,5},{5,6},{6,7},{7,4},{8,9},{9,10},{10,1... | collective-permute-start | bytes 3145736 | tf_op jit(solution)/shard_map/ppermute | solution.py:25
  29.5 0.0 collective-permute-start.5
  29.5 5.8 %collective-permute-done.3.refs_4_ = bf16[2,2,64,1024]{3,2,1,0:T(8,128)(2,1)S(1)} collective-permute-done((bf16[2,2,64,1024]{3,2,1,0:T(8,128)(2,1)}, bf16[2,2,64,1024]{3,2,1,0:T(8,128)(2,1)S(1)}, u32[]{:S(2)}, u32[]{:S(2)}) %collective-permute-start.3) | collective-permute-done | bytes 524320 | tf_op jit(solution)/shard_map/ppermute | solution.py:25
  35.3 3.0 %collective-permute-start.4 = (bf16[1,2,64,1024]{3,2,1,0:T(8,128)(2,1)S(1)}, bf16[1,2,64,1024]{3,2,1,0:T(8,128)(2,1)S(1)}, u32[]{:S(2)}, u32[]{:S(2)}) collective-permute-start(bf16[1,2,64,1024]{3,2,1,0:T(8,128)(2,1)S(1)} %slice.4), channel_id=1, source_target_pairs={{0,32},{1,33},{2,34},{3,35},{4,36},{5,37},{6,38},{7,39},{8,40},{9,... | collective-permute-start | bytes 786440 | tf_op jit(solution)/shard_map/ppermute | solution.py:25
  38.4 0.3 collective-permute-start.6
  38.7 0.8 %copy-done = bf16[2,2,64,1024]{3,2,1,0:T(8,128)(2,1)} copy-done((bf16[2,2,64,1024]{3,2,1,0:T(8,128)(2,1)}, bf16[2,2,64,1024]{3,2,1,0:T(8,128)(2,1)S(1)}, u32[]{:S(2)}) %copy-start) | copy-done | bytes 524312
  39.4 0.2 collective-permute-start.7
  39.7 2.6 %collective-permute-start.14 = (bf16[4,2,64,1024]{3,2,1,0:T(8,128)(2,1)}, bf16[4,2,64,1024]{3,2,1,0:T(8,128)(2,1)S(1)}, u32[]{:S(2)}, u32[]{:S(2)}) collective-permute-start(bf16[4,2,64,1024]{3,2,1,0:T(8,128)(2,1)} %pad_maximum_fusion.refs_10_), channel_id=1, source_target_pairs={{0,2},{1,3},{2,0},{3,1},{4,6},{5,7},{6,4},{7,5},{8,10},{9,11},{10,... | collective-permute-start | bytes 3145736 | tf_op jit(solution)/shard_map/ppermute | solution.py:25
  42.3 3.8 %collective-permute-start.8 = (bf16[1,2,64,1024]{3,2,1,0:T(8,128)(2,1)S(1)}, bf16[1,2,64,1024]{3,2,1,0:T(8,128)(2,1)S(1)}, u32[]{:S(2)}, u32[]{:S(2)}) collective-permute-start(bf16[1,2,64,1024]{3,2,1,0:T(8,128)(2,1)S(1)} %collective-permute-done.4.refs_5_), channel_id=1, source_target_pairs={{0,16},{1,17},{2,18},{3,19},{4,20},{5,21},{6,22},{7,23},{8,24},{9,... | collective-permute-start | bytes 786440 | tf_op jit(solution)/shard_map/ppermute | solution.py:25
  46.1 0.1 stack.91
  46.3 1.0 %collective-permute-done.8.refs_9_ = bf16[1,2,64,1024]{3,2,1,0:T(8,128)(2,1)S(1)} collective-permute-done((bf16[1,2,64,1024]{3,2,1,0:T(8,128)(2,1)S(1)}, bf16[1,2,64,1024]{3,2,1,0:T(8,128)(2,1)S(1)}, u32[]{:S(2)}, u32[]{:S(2)}) %collective-permute-start.8) | collective-permute-done | bytes 262176 | tf_op jit(solution)/shard_map/ppermute | solution.py:25
  47.3 0.7 %copy-done.2 = bf16[1,2,64,1024]{3,2,1,0:T(8,128)(2,1)} copy-done((bf16[1,2,64,1024]{3,2,1,0:T(8,128)(2,1)}, bf16[1,2,64,1024]{3,2,1,0:T(8,128)(2,1)S(1)}, u32[]{:S(2)}) %copy-start.2) | copy-done | bytes 262168
  48.0 1.0 %copy-done.1 = bf16[2,2,64,1024]{3,2,1,0:T(8,128)(2,1)S(1)} copy-done((bf16[2,2,64,1024]{3,2,1,0:T(8,128)(2,1)S(1)}, bf16[2,2,64,1024]{3,2,1,0:T(8,128)(2,1)}, u32[]{:S(2)}) %copy-start.1) | copy-done | bytes 524312
  49.1 0.9 %copy-done.3 = bf16[1,2,64,1024]{3,2,1,0:T(8,128)(2,1)S(1)} copy-done((bf16[1,2,64,1024]{3,2,1,0:T(8,128)(2,1)S(1)}, bf16[1,2,64,1024]{3,2,1,0:T(8,128)(2,1)}, u32[]{:S(2)}) %copy-start.3) | copy-done | bytes 262168
  50.0 10.6 %shard_map.28 = (f32[2,1024,1024]{2,1,0:T(8,128)S(1)}, bf16[4,2,64,1024]{3,2,1,0:T(8,128)(2,1)S(1)}) custom-call(s32[16]{0:T(128)S(1)} %fusion.2.refs_0_, bf16[2,2,64,1024]{3,2,1,0:T(8,128)(2,1)S(1)} %pad_maximum_fusion.1.refs_1_, bf16[2,2,64,1024]{3,2,1,0:T(8,128)(2,1)S(1)} %collective-permute-done.1.refs_2_, ...), custom_call_target="tpu_custom_call" | custom-call | flops 6442450944 | bytes 8388608 | tf_op jit(solution)/shard_map/pallas_call | solution.py:88
  60.7 6.5 %shard_map.29 = f32[2,1024,1024]{2,1,0:T(8,128)} custom-call(f32[2,1024,1024]{2,1,0:T(8,128)S(1)} %get-tuple-element.7.acc, bf16[4,2,64,1024]{3,2,1,0:T(8,128)(2,1)S(1)} %get-tuple-element.8.right, bf16[4,2,64,1024]{3,2,1,0:T(8,128)(2,1)S(1)} %collective-permute-done.14.left), custom_call_target="tpu_custom_call" | custom-call | flops 2147483648 | bytes 9437184 | tf_op jit(solution)/shard_map/pallas_call | solution.py:119
  (15 shorter events, 0.1 us)
Async XLA Ops:
  0.0 4.6 %collective-permute-start = (bf16[2,64,1024]{2,1,0:T(8,128)(2,1)}, bf16[2,64,1024]{2,1,0:T(8,128)(2,1)S(1)}, u32[]{:S(2)}, u32[]{:S(2)}) collective-permute-start(bf16[2,64,1024]{2,1,0:T(8,128)(2,1)} %param.3), channel_id=1, source_target_pairs={{0,16},{1,17},{2,18},{3,19},{4,20},{5,21},{6,22},{7,23},{8,24},{9,... | collective-permute-start | bytes 786440 | tf_op jit(solution)/shard_map/ppermute | solution.py:25
  5.6 10.0 %collective-permute-start.1 = (bf16[2,2,64,1024]{3,2,1,0:T(8,128)(2,1)S(1)}, bf16[2,2,64,1024]{3,2,1,0:T(8,128)(2,1)S(1)}, u32[]{:S(2)}, u32[]{:S(2)}) collective-permute-start(bf16[2,2,64,1024]{3,2,1,0:T(8,128)(2,1)S(1)} %pad_maximum_fusion.1.refs_1_), channel_id=1, source_target_pairs={{0,32},{1,33},{2,34},{3,35},{4,36},{5,37},{6,38},{7,39},{8,40},{9,... | collective-permute-start | bytes 1572872 | tf_op jit(solution)/shard_map/ppermute | solution.py:25
  9.5 9.5 %collective-permute-start.10 = (bf16[2,64,1024]{2,1,0:T(8,128)(2,1)}, bf16[2,64,1024]{2,1,0:T(8,128)(2,1)S(1)}, u32[]{:S(2)}, u32[]{:S(2)}) collective-permute-start(bf16[2,64,1024]{2,1,0:T(8,128)(2,1)} %bitcast.26), channel_id=1, source_target_pairs={{0,12},{1,13},{2,14},{3,15},{4,0},{5,1},{6,2},{7,3},{8,4},{9,5},{1... | collective-permute-start | bytes 786440 | tf_op jit(solution)/shard_map/ppermute | solution.py:25
  12.3 9.9 %collective-permute-start.9 = (bf16[2,64,1024]{2,1,0:T(8,128)(2,1)}, bf16[2,64,1024]{2,1,0:T(8,128)(2,1)S(1)}, u32[]{:S(2)}, u32[]{:S(2)}) collective-permute-start(bf16[2,64,1024]{2,1,0:T(8,128)(2,1)} %bitcast.27), channel_id=1, source_target_pairs={{0,4},{1,5},{2,6},{3,7},{4,8},{5,9},{6,10},{7,11},{8,12},{9,13},{1... | collective-permute-start | bytes 786440 | tf_op jit(solution)/shard_map/ppermute | solution.py:25
  12.3 9.9 %collective-permute-start.11 = (bf16[2,64,1024]{2,1,0:T(8,128)(2,1)}, bf16[2,64,1024]{2,1,0:T(8,128)(2,1)S(1)}, u32[]{:S(2)}, u32[]{:S(2)}) collective-permute-start(bf16[2,64,1024]{2,1,0:T(8,128)(2,1)} %bitcast.28), channel_id=1, source_target_pairs={{0,8},{1,9},{2,10},{3,11},{4,12},{5,13},{6,14},{7,15},{8,0},{9,1},... | collective-permute-start | bytes 786440 | tf_op jit(solution)/shard_map/ppermute | solution.py:25
  15.7 11.0 %collective-permute-start.2 = (bf16[2,2,64,1024]{3,2,1,0:T(8,128)(2,1)S(1)}, bf16[2,2,64,1024]{3,2,1,0:T(8,128)(2,1)}, u32[]{:S(2)}, u32[]{:S(2)}) collective-permute-start(bf16[2,2,64,1024]{3,2,1,0:T(8,128)(2,1)S(1)} %collective-permute-done.1.refs_2_), channel_id=1, source_target_pairs={{0,32},{1,33},{2,34},{3,35},{4,36},{5,37},{6,38},{7,39},{8,40},{9,... | collective-permute-start | bytes 1572872 | tf_op jit(solution)/shard_map/ppermute | solution.py:25
  24.2 15.5 %collective-permute-start.13 = (bf16[4,2,64,1024]{3,2,1,0:T(8,128)(2,1)}, bf16[4,2,64,1024]{3,2,1,0:T(8,128)(2,1)S(1)}, u32[]{:S(2)}, u32[]{:S(2)}) collective-permute-start(bf16[4,2,64,1024]{3,2,1,0:T(8,128)(2,1)} %pad_maximum_fusion.refs_10_), channel_id=1, source_target_pairs={{0,3},{1,0},{2,1},{3,2},{4,7},{5,4},{6,5},{7,6},{8,11},{9,8},{10,9... | collective-permute-start | bytes 3145736 | tf_op jit(solution)/shard_map/ppermute | solution.py:25
  26.7 8.6 %collective-permute-start.3 = (bf16[2,2,64,1024]{3,2,1,0:T(8,128)(2,1)}, bf16[2,2,64,1024]{3,2,1,0:T(8,128)(2,1)S(1)}, u32[]{:S(2)}, u32[]{:S(2)}) collective-permute-start(bf16[2,2,64,1024]{3,2,1,0:T(8,128)(2,1)} %collective-permute-done.2.refs_3_), channel_id=1, source_target_pairs={{0,32},{1,33},{2,34},{3,35},{4,36},{5,37},{6,38},{7,39},{8,40},{9,... | collective-permute-start | bytes 1572872 | tf_op jit(solution)/shard_map/ppermute | solution.py:25
  28.4 17.8 %collective-permute-start.12 = (bf16[4,2,64,1024]{3,2,1,0:T(8,128)(2,1)}, bf16[4,2,64,1024]{3,2,1,0:T(8,128)(2,1)}, u32[]{:S(2)}, u32[]{:S(2)}) collective-permute-start(bf16[4,2,64,1024]{3,2,1,0:T(8,128)(2,1)} %pad_maximum_fusion.refs_10_), channel_id=1, source_target_pairs={{0,1},{1,2},{2,3},{3,0},{4,5},{5,6},{6,7},{7,4},{8,9},{9,10},{10,1... | collective-permute-start | bytes 3145736 | tf_op jit(solution)/shard_map/ppermute | solution.py:25
  29.5 9.2 %collective-permute-start.5 = (bf16[2,2,64,1024]{3,2,1,0:T(8,128)(2,1)S(1)}, bf16[2,2,64,1024]{3,2,1,0:T(8,128)(2,1)S(1)}, u32[]{:S(2)}, u32[]{:S(2)}) collective-permute-start(bf16[2,2,64,1024]{3,2,1,0:T(8,128)(2,1)S(1)} %collective-permute-done.1.refs_2_), channel_id=1, source_target_pairs={{0,16},{1,17},{2,18},{3,19},{4,20},{5,21},{6,22},{7,23},{8,24},{9,... | collective-permute-start | bytes 1572872 | tf_op jit(solution)/shard_map/ppermute | solution.py:25
  35.3 7.0 %collective-permute-start.4 = (bf16[1,2,64,1024]{3,2,1,0:T(8,128)(2,1)S(1)}, bf16[1,2,64,1024]{3,2,1,0:T(8,128)(2,1)S(1)}, u32[]{:S(2)}, u32[]{:S(2)}) collective-permute-start(bf16[1,2,64,1024]{3,2,1,0:T(8,128)(2,1)S(1)} %slice.4), channel_id=1, source_target_pairs={{0,32},{1,33},{2,34},{3,35},{4,36},{5,37},{6,38},{7,39},{8,40},{9,... | collective-permute-start | bytes 786440 | tf_op jit(solution)/shard_map/ppermute | solution.py:25
  38.4 7.9 %collective-permute-start.6 = (bf16[2,2,64,1024]{3,2,1,0:T(8,128)(2,1)}, bf16[2,2,64,1024]{3,2,1,0:T(8,128)(2,1)}, u32[]{:S(2)}, u32[]{:S(2)}) collective-permute-start(bf16[2,2,64,1024]{3,2,1,0:T(8,128)(2,1)} %collective-permute-done.2.refs_3_), channel_id=1, source_target_pairs={{0,16},{1,17},{2,18},{3,19},{4,20},{5,21},{6,22},{7,23},{8,24},{9,... | collective-permute-start | bytes 1572872 | tf_op jit(solution)/shard_map/ppermute | solution.py:25
  38.7 0.8 %copy-start = (bf16[2,2,64,1024]{3,2,1,0:T(8,128)(2,1)}, bf16[2,2,64,1024]{3,2,1,0:T(8,128)(2,1)S(1)}, u32[]{:S(2)}) copy-start(bf16[2,2,64,1024]{3,2,1,0:T(8,128)(2,1)S(1)} %collective-permute-done.5.refs_6_) | copy-start | bytes 1572868
  39.4 8.6 %collective-permute-start.7 = (bf16[2,2,64,1024]{3,2,1,0:T(8,128)(2,1)S(1)}, bf16[2,2,64,1024]{3,2,1,0:T(8,128)(2,1)}, u32[]{:S(2)}, u32[]{:S(2)}) collective-permute-start(bf16[2,2,64,1024]{3,2,1,0:T(8,128)(2,1)S(1)} %collective-permute-done.3.refs_4_), channel_id=1, source_target_pairs={{0,16},{1,17},{2,18},{3,19},{4,20},{5,21},{6,22},{7,23},{8,24},{9,... | collective-permute-start | bytes 1572872 | tf_op jit(solution)/shard_map/ppermute | solution.py:25
  39.7 2.6 %copy-start.4 = (bf16[4,2,64,1024]{3,2,1,0:T(8,128)(2,1)}, bf16[4,2,64,1024]{3,2,1,0:T(8,128)(2,1)S(1)}, u32[]{:S(2)}) copy-start(bf16[4,2,64,1024]{3,2,1,0:T(8,128)(2,1)S(1)} %collective-permute-done.13.refs_12_) | copy-start | bytes 3145732
  39.7 21.0 %collective-permute-start.14 = (bf16[4,2,64,1024]{3,2,1,0:T(8,128)(2,1)}, bf16[4,2,64,1024]{3,2,1,0:T(8,128)(2,1)S(1)}, u32[]{:S(2)}, u32[]{:S(2)}) collective-permute-start(bf16[4,2,64,1024]{3,2,1,0:T(8,128)(2,1)} %pad_maximum_fusion.refs_10_), channel_id=1, source_target_pairs={{0,2},{1,3},{2,0},{3,1},{4,6},{5,7},{6,4},{7,5},{8,10},{9,11},{10,... | collective-permute-start | bytes 3145736 | tf_op jit(solution)/shard_map/ppermute | solution.py:25
  42.3 5.0 %collective-permute-start.8 = (bf16[1,2,64,1024]{3,2,1,0:T(8,128)(2,1)S(1)}, bf16[1,2,64,1024]{3,2,1,0:T(8,128)(2,1)S(1)}, u32[]{:S(2)}, u32[]{:S(2)}) collective-permute-start(bf16[1,2,64,1024]{3,2,1,0:T(8,128)(2,1)S(1)} %collective-permute-done.4.refs_5_), channel_id=1, source_target_pairs={{0,16},{1,17},{2,18},{3,19},{4,20},{5,21},{6,22},{7,23},{8,24},{9,... | collective-permute-start | bytes 786440 | tf_op jit(solution)/shard_map/ppermute | solution.py:25
  47.3 0.7 %copy-start.2 = (bf16[1,2,64,1024]{3,2,1,0:T(8,128)(2,1)}, bf16[1,2,64,1024]{3,2,1,0:T(8,128)(2,1)S(1)}, u32[]{:S(2)}) copy-start(bf16[1,2,64,1024]{3,2,1,0:T(8,128)(2,1)S(1)} %collective-permute-done.8.refs_9_) | copy-start | bytes 786436
  48.0 1.0 %copy-start.1 = (bf16[2,2,64,1024]{3,2,1,0:T(8,128)(2,1)S(1)}, bf16[2,2,64,1024]{3,2,1,0:T(8,128)(2,1)}, u32[]{:S(2)}) copy-start(bf16[2,2,64,1024]{3,2,1,0:T(8,128)(2,1)} %copy-done) | copy-start | bytes 1572868
  49.1 0.9 %copy-start.3 = (bf16[1,2,64,1024]{3,2,1,0:T(8,128)(2,1)S(1)}, bf16[1,2,64,1024]{3,2,1,0:T(8,128)(2,1)}, u32[]{:S(2)}) copy-start(bf16[1,2,64,1024]{3,2,1,0:T(8,128)(2,1)} %copy-done.2) | copy-start | bytes 786436

commit v2 on v0

v2 whole, which is shorter than its diff:
```python
import jax
import jax.numpy as jnp
from jax import lax
from jax.experimental import pallas as pl
from jax.experimental.pallas import tpu as pltpu
from jax.sharding import PartitionSpec as P

AXES = ("row", "col")
RING = (0, -1, 1, 2)


def permute(value, target):
    pairs = []
    for z in range(8):
        for core in range(2):
            for x in range(4):
                for y in range(4):
                    to_z, to_core, to_x, to_y = target(z, core, x, y)
                    pairs.append(
                        (
                            (z * 2 + core) * 16 + x * 4 + y,
                            (to_z % 8 * 2 + to_core) * 16 + to_x % 4 * 4 + to_y % 4,
                        )
                    )
    return lax.ppermute(value, AXES, pairs)


def first_axis(step):
    return lambda z, c, x, y: (z, c, x + step, y) if c == 0 else (z, c, x, y + step)


def second_axis(step):
    return lambda z, c, x, y: (z, c, x, y + step) if c == 0 else (z, c, x + step, y)


def along_z(step):
    return lambda z, c, x, y: (z + step, c, x, y) if c == 0 else (z - step, c, x, y)


def other_core(z, c, x, y):
    return (z, 1 - c, x, y)


VMEM = pl.BlockSpec(memory_space=pltpu.VMEM)
SMEM = pl.BlockSpec(memory_space=pltpu.SMEM)
MIB = 2**20


def on_chip(*values):
    return [pltpu.with_memory_space_constraint(value, pltpu.VMEM) for value in values]


def limit(mib):
    return pltpu.CompilerParams(vmem_limit_bytes=mib * MIB)


def cost(flops, moved):
    return pl.CostEstimate(flops=flops, bytes_accessed=moved, transcendentals=0)


ANY = pl.BlockSpec(memory_space=pl.ANY)
HBM = pl.BlockSpec(memory_space=pltpu.HBM)
RIGHT = pltpu.VMEM((4, 2, 4, 64, 1024), jnp.bfloat16)


def in_hbm(value):
    return pltpu.with_memory_space_constraint(value, pltpu.HBM)


def slot_of(right, places, slot):
    at = places[slot]
    return right.at[at // 4, :, at % 4]


def stack_kernel(own, *refs):
    parts, out, sem = refs[:-2], refs[-2], refs[-1]
    copy = pltpu.make_async_copy(own, out.at[0], sem)
    copy.start()
    for i, part in enumerate(parts):
        out[i + 1] = part[...]
    copy.wait()


def stack(own, *parts):
    n = len(parts)
    return pl.pallas_call(
        stack_kernel,
        out_shape=pltpu.VMEM((n + 1, *own.shape), own.dtype),
        in_specs=[HBM] + [VMEM] * n,
        out_specs=VMEM,
        scratch_shapes=[pltpu.SemaphoreType.DMA],
        compiler_params=limit(2),
        cost_estimate=cost(0, 2 * MIB),
    )(in_hbm(own), *on_chip(*parts))


def first_kernel(places, mine, swapped, back, *refs):
    right, sem = refs[-2:]
    copy = pltpu.make_async_copy(mine, slot_of(right, places, 0), sem)
    copy.start()
    slot_of(right, places, 1)[...] = swapped[...]
    slot_of(right, places, 2)[...] = back[...]
    for slot in (FAR, FAR + 1):
        slot_of(right, places, slot)[...] = jnp.zeros((2, 64, 1024), jnp.bfloat16)
    copy.wait()


def first(places, mine, swapped, back, *others):
    return pl.pallas_call(
        first_kernel,
        out_shape=RIGHT,
        in_specs=[SMEM, HBM] + [VMEM] * 2 + [ANY] * len(others),
        out_specs=VMEM,
        scratch_shapes=[pltpu.SemaphoreType.DMA],
        compiler_params=limit(3),
        cost_estimate=cost(0, 2 * MIB),
    )(places, in_hbm(mine), *on_chip(swapped, back), *others)


def after(values, *others):
    n = len(values)
    return pl.pallas_call(
        lambda *refs: None,
        out_shape=[jax.ShapeDtypeStruct(v.shape, v.dtype) for v in values],
        in_specs=[ANY] * (n + len(others)),
        out_specs=[ANY] * n,
        input_output_aliases={i: i for i in range(n)},
        compiler_params=limit(1),
        cost_estimate=cost(0, 0),
    )(*values, *others)


def place_kernel(slots, places, *refs):
    right, sems = refs[-2:]
    copies = [
        pltpu.make_async_copy(part, slot_of(right, places, slot), sems.at[i])
        for i, (part, slot) in enumerate(zip(refs, slots))
    ]
    for copy in copies:
        copy.start()
    for copy in copies:
        copy.wait()


def place(right, slots, parts, places):
    n = len(parts)
    return pl.pallas_call(
        lambda *refs: place_kernel(slots, *refs),
        out_shape=RIGHT,
        in_specs=[SMEM] + [ANY] * (n + 1),
        out_specs=ANY,
        scratch_shapes=[pltpu.SemaphoreType.DMA((n,))],
        input_output_aliases={n + 1: 0},
        compiler_params=limit(1),
        cost_estimate=cost(0, MIB // 2),
    )(places, *parts, *on_chip(right))


def turned(left, rows):
    sides = []
    for plane in range(2):
        side = jnp.concatenate([part[:, plane, :, rows] for part in left])
        sides.append(side.reshape(side.shape[0] * 64, 256).T)
    return jnp.concatenate([sides[0], -sides[1]], 1), jnp.concatenate(sides[::-1], 1)


def turn_kernel(left, real, imag):
    for m in range(0, 1024, 256):
        rows = slice(m, m + 256)
        real[rows], imag[rows] = turned([left], rows)


def turn(left):
    out = pltpu.VMEM((1024, 512), jnp.bfloat16)
    return pl.pallas_call(
        turn_kernel,
        out_shape=[out, out],
        in_specs=[VMEM],
        out_specs=[VMEM] * 2,
        compiler_params=limit(6),
        cost_estimate=cost(0, 3 * MIB),
    )(*on_chip(left))


def early_kernel(right, *refs):
    reals, imags, acc = refs[0:6:2], refs[1:6:2], refs[6]

    @pl.loop(0, 4)
    def _(t):
        n = pl.ds(pl.multiple_of(t * 256, 256), 256)
        columns = right[0:3, :, :, :, n].reshape(1536, 256)
        for plane, sides in enumerate((reals, imags)):
            rows = jnp.concatenate([side[...] for side in sides], 1)
            acc[plane, :, n] = jnp.dot(rows, columns, preferred_element_type=jnp.float32)


def early(right, sides):
    return pl.pallas_call(
        early_kernel,
        out_shape=pltpu.VMEM((2, 1024, 1024), jnp.float32),
        in_specs=[VMEM] * 7,
        out_specs=VMEM,
        compiler_params=limit(8),
        cost_estimate=cost(6 * 2**30, 8 * MIB),
    )(*on_chip(right, *sides))


def late_kernel(places, acc, right, far_own, far_swapped, ring, back, ahead, up, down, out, extra):
    @pl.when(pl.program_id(0) == 0)
    def _():
        for i in range(2):
            at = places[14 + i]
            for g, group in enumerate((ring, back, ahead)):

                @pl.when(at // 4 == g)
                def _():
                    extra[i] = group[at % 4]

            @pl.when((at // 4 == 3) & (at % 4 < 2))
            def _():
                extra[i] = up[at % 2]

            @pl.when((at // 4 == 3) & (at % 4 >= 2))
            def _():
                extra[i] = down[at % 2]

    m = pl.ds(pl.multiple_of(pl.program_id(0) * 256, 256), 256)
    real, imag = turned([up, down, extra], m)
    columns = jnp.concatenate(
        [
            block
            for plane in range(2)
            for block in (right[3, plane].reshape(256, 1024), far_own[plane], far_swapped[plane])
        ]
    )
    out[0] = acc[0, m] + jnp.dot(real, columns, preferred_element_type=jnp.float32)
    out[1] = acc[1, m] + jnp.dot(imag, columns, preferred_element_type=jnp.float32)


def late(places, acc, right, far, groups, up, down):
    return pl.pallas_call(
        late_kernel,
        grid=(4,),
        out_shape=jax.ShapeDtypeStruct((2, 1024, 1024), jnp.float32),
        in_specs=[SMEM] + [VMEM] * 9,
        out_specs=pl.BlockSpec((2, 256, 1024), lambda i: (0, i, 0)),
        scratch_shapes=[pltpu.VMEM((2, 2, 64, 1024), jnp.bfloat16)],
        compiler_params=limit(14),
        cost_estimate=cost(3 * 2**30, 9 * MIB),
    )(places, *on_chip(acc, right, *far, *groups, up, down))


def right_places(offsets):
    row, col = lax.axis_index("row"), lax.axis_index("col")
    z, core, x, y = row // 2, row % 2, col // 4, col % 4
    sign = 1 - 2 * core
    trace = []
    for steps, shard, by in offsets:
        holder = core if by == 0 else 1 - core
        way = sign if by == 0 else -sign
        trace.append((z - way * steps) % 8 * 2 + (holder if shard == 0 else 1 - holder))
    trace = jnp.stack(trace)
    dx, dy = (trace // 4 - x) % 4, (trace % 4 - y) % 4
    member = jnp.where(core == 0, dx, dy)
    group = jnp.where(core == 0, dy, dx)
    order = lambda d: jnp.where(d == 3, 1, jnp.where(d == 1, 2, jnp.where(d == 2, 3, 0)))
    return (order(group) * 4 + order(member)).astype(jnp.int32)


BLOCKS = [(0, 0, 0), (0, 1, 0)]
BLOCKS += [(step, shard, by) for step in range(1, 4) for shard in range(2) for by in range(2)]
BLOCKS += [(4, 0, 0), (4, 0, 1)]
FAR = 14


def local(left_panel, right_panel):
    own = jnp.swapaxes(left_panel, 1, 2)
    places = right_places(BLOCKS)
    swapped = permute(right_panel, other_core)
    near = [permute(own, first_axis(d)) for d in (1, -1, 2)]
    ring = stack(own, *near)
    back = permute(ring, second_axis(1))
    ahead = permute(ring, second_axis(-1))
    far_back = permute(back[:2], second_axis(1))
    far_ahead = permute(ahead[2:], second_axis(-1))

    held = [right_panel, swapped]
    waiting = []
    for slot in range(2, FAR, 2):
        step, shard, _ = BLOCKS[slot]
        part = permute(held[shard], along_z(1))
        if slot == 2:
            right = first(places, right_panel, swapped, part, ring)
        else:
            due = waiting[:1] if slot < 12 else waiting[:1]
            waiting = waiting[1:]
            right = place(right, [slot] + [s for s, _ in due], [part] + [p for _, p in due], places)
        part, = after((part,), right)
        held[shard] = part
        waiting.append((slot + 1, permute(part, other_core)))
    far = permute(held[0], along_z(1))
    right = place(right, [s for s, _ in waiting], [p for _, p in waiting], places)

    groups = (ring, back, ahead)
    acc = early(right, [side for group in groups for side in turn(group)])
    far, = after((far,), acc)
    return late(places, acc, right, (far, permute(far, other_core)), groups, far_back, far_ahead)


def solution(mesh):
    placed = (P(None, "row", "col"), P(None, "row", "col"))
    return jax.shard_map(
        local, mesh=mesh, in_specs=placed, out_specs=P(None, "row", "col"), check_vma=False
    )
```

time: 138 us -> 62.7 us (0.45)
  waiting for transfers between devices: 108 us -> 5.84 us
  starting transfers between devices: 0.04 us -> 35.6 us
  Pallas kernels: 0 us -> 20.7 us
  between operations: 13.4 us -> 0.23 us
  matrix products: 12.3 us -> 0 us
  other arithmetic: 4.24 us -> 0.02 us
    all_gather x2 -> x0, waiting for transfers between devices: 106 us -> none  [the longest x1 62.3 us: local(): left_all = lax.all_gather(left_panel, 'col', axis=2, tiled=True)]
    ppermute x0 -> x22, starting transfers between devices: none -> 35.6 us  [permute(): return lax.ppermute(value, AXES, pairs)]
    pallas_call x0 -> x20, Pallas kernels: none -> 20.7 us  [the longest x1 7.14 us: early(): pl.pallas_call(early_kernel, out_shape=pltpu.VMEM((2, 1024, 1024), jnp.fl...]
    dot_general x4 -> x0, matrix products: 12.3 us -> none  [the longest x1 4.75 us: complex_block(): jnp.dot(left_real, right_imag, preferred_element_type=jnp.float32)]
    ppermute x0 -> x22, waiting for transfers between devices: none -> 5.84 us  [permute(): return lax.ppermute(value, AXES, pairs)]
    another operation x1 -> x0, other arithmetic: 4.24 us -> none  [complex_block(): return jnp.stack([real_part, imag_part])]
    unnamed x2 -> x0, waiting for transfers between devices: 1.41 us -> none
  transfers between devices with their start and end apart: 2 -> 22, of which waited for: 2 -> 6; matrix products, arithmetic and copies ran while one was open for 0% -> 0% of each run, Pallas kernels for 0% -> 23%
where the time goes in v2:
time: 62.7 us; the launch traced here: 62.6 us
  starting transfers between devices  35.6 us (57%)
  Pallas kernels  20.7 us (33%)
  waiting for transfers between devices  5.84 us (9%)
    ppermute x22, starting transfers between devices, permute(): return lax.ppermute(value, AXES, pairs)  35.6 us
    pallas_call x1, Pallas kernels, early(): pl.pallas_call(early_kernel, out_shape=pltpu.VMEM((2, 1024, 1024), jnp.fl...  7.14 us
    pallas_call x1, Pallas kernels, late(): pl.pallas_call(late_kernel, grid=(4,), out_shape=jax.ShapeDtypeStruct((2,...  6.47 us
    ppermute x22, waiting for transfers between devices, permute(): return lax.ppermute(value, AXES, pairs)  5.84 us
    pallas_call x6, Pallas kernels, place(): pl.pallas_call(lambda *refs: place_kernel(slots, *refs), out_shape=RIGHT,...  3.66 us
    pallas_call x1, Pallas kernels, first(): pl.pallas_call(first_kernel, out_shape=RIGHT, in_specs=[SMEM, HBM] + [VME...  1.51 us
  transfers between devices with their start and end apart: 22, of which 6 were waited for; matrix products, arithmetic and copies ran while one was open for 0% of the time, Pallas kernels for 23%

profile of v2, /device:TPU:1, one launch (start us, length us, event | category | flops | bytes accessed | tf_op | source)
XLA Modules:
  0.0 62.6 jit_solution(6967473455994932798)
XLA Ops:
  0.0 3.2 %collective-permute-start = (bf16[2,64,1024]{2,1,0:T(8,128)(2,1)}, bf16[2,64,1024]{2,1,0:T(8,128)(2,1)S(1)}, u32[]{:S(2)}, u32[]{:S(2)}) collective-permute-start(bf16[2,64,1024]{2,1,0:T(8,128)(2,1)} %mine.1), channel_id=1, source_target_pairs={{0,16},{1,17},{2,18},{3,19},{4,20},{5,21},{6,22},{7,23},{8,24},{9,... | collective-permute-start | bytes 786440 | tf_op jit(solution)/shard_map/ppermute | solution.py:25
  3.2 1.2 %collective-permute-start.5 = (bf16[2,64,1024]{2,1,0:T(8,128)(2,1)}, bf16[2,64,1024]{2,1,0:T(8,128)(2,1)S(1)}, u32[]{:S(2)}, u32[]{:S(2)}) collective-permute-start(bf16[2,64,1024]{2,1,0:T(8,128)(2,1)} %bitcast.17), channel_id=1, source_target_pairs={{0,8},{1,9},{2,10},{3,11},{4,12},{5,13},{6,14},{7,15},{8,0},{9,1},... | collective-permute-start | bytes 786440 | tf_op jit(solution)/shard_map/ppermute | solution.py:25
  4.4 0.8 %collective-permute-start.4 = (bf16[2,64,1024]{2,1,0:T(8,128)(2,1)}, bf16[2,64,1024]{2,1,0:T(8,128)(2,1)S(1)}, u32[]{:S(2)}, u32[]{:S(2)}) collective-permute-start(bf16[2,64,1024]{2,1,0:T(8,128)(2,1)} %bitcast.18), channel_id=1, source_target_pairs={{0,12},{1,13},{2,14},{3,15},{4,0},{5,1},{6,2},{7,3},{8,4},{9,5},{1... | collective-permute-start | bytes 786440 | tf_op jit(solution)/shard_map/ppermute | solution.py:25
  5.2 0.7 %collective-permute-start.3 = (bf16[2,64,1024]{2,1,0:T(8,128)(2,1)}, bf16[2,64,1024]{2,1,0:T(8,128)(2,1)S(1)}, u32[]{:S(2)}, u32[]{:S(2)}) collective-permute-start(bf16[2,64,1024]{2,1,0:T(8,128)(2,1)} %bitcast.19), channel_id=1, source_target_pairs={{0,4},{1,5},{2,6},{3,7},{4,8},{5,9},{6,10},{7,11},{8,12},{9,13},{1... | collective-permute-start | bytes 786440 | tf_op jit(solution)/shard_map/ppermute | solution.py:25
  5.9 5.6 %collective-permute-start.2 = (bf16[2,64,1024]{2,1,0:T(8,128)(2,1)}, bf16[2,64,1024]{2,1,0:T(8,128)(2,1)S(1)}, u32[]{:S(2)}, u32[]{:S(2)}) collective-permute-start(bf16[2,64,1024]{2,1,0:T(8,128)(2,1)} %mine.1), channel_id=1, source_target_pairs={{0,32},{1,33},{2,34},{3,35},{4,36},{5,37},{6,38},{7,39},{8,40},{9,... | collective-permute-start | bytes 786440 | tf_op jit(solution)/shard_map/ppermute | solution.py:25
  11.6 0.8 %collective-permute-start.1 = (bf16[2,64,1024]{2,1,0:T(8,128)(2,1)S(1)}, bf16[2,64,1024]{2,1,0:T(8,128)(2,1)S(1)}, u32[]{:S(2)}, u32[]{:S(2)}) collective-permute-start(bf16[2,64,1024]{2,1,0:T(8,128)(2,1)S(1)} %collective-permute-done.swapped), channel_id=1, source_target_pairs={{0,32},{1,33},{2,34},{3,35},{4,36},{5,37},{6,38},{7,39},{8,40},{9,... | collective-permute-start | bytes 786440 | tf_op jit(solution)/shard_map/ppermute | solution.py:25
  12.4 0.9 %collective-permute-done.3.refs_0_ = bf16[2,64,1024]{2,1,0:T(8,128)(2,1)S(1)} collective-permute-done((bf16[2,64,1024]{2,1,0:T(8,128)(2,1)}, bf16[2,64,1024]{2,1,0:T(8,128)(2,1)S(1)}, u32[]{:S(2)}, u32[]{:S(2)}) %collective-permute-start.3) | collective-permute-done | bytes 262176 | tf_op jit(solution)/shard_map/ppermute | solution.py:25
  13.3 1.0 %shard_map.28.refs_0_.left.ring = bf16[4,2,64,1024]{3,2,1,0:T(8,128)(2,1)S(1)} custom-call(bf16[2,64,1024]{2,1,0:T(8,128)(2,1)} %bitcast.20, bf16[2,64,1024]{2,1,0:T(8,128)(2,1)S(1)} %collective-permute-done.3.refs_0_, bf16[2,64,1024]{2,1,0:T(8,128)(2,1)S(1)} %collective-permute-done.4.refs_1_, bf16[2,64,1024]{2,1,0:T(8,128)(2,1)S(1)} %collective-permute-done.5.refs_2_), custom_call_target="tpu_custom_call" | custom-call | bytes 2097152 | tf_op jit(solution)/shard_map/pallas_call | solution.py:86
  14.2 0.8 %collective-permute-done.2.back.refs_0_ = bf16[2,64,1024]{2,1,0:T(8,128)(2,1)S(1)} collective-permute-done((bf16[2,64,1024]{2,1,0:T(8,128)(2,1)}, bf16[2,64,1024]{2,1,0:T(8,128)(2,1)S(1)}, u32[]{:S(2)}, u32[]{:S(2)}) %collective-permute-start.2) | collective-permute-done | bytes 262176 | tf_op jit(solution)/shard_map/ppermute | solution.py:25
  15.1 1.5 %shard_map.29.refs_1_.refs_3_ = bf16[4,2,4,64,1024]{4,3,2,1,0:T(8,128)(2,1)S(1)} custom-call(s32[16]{0:T(128)S(1)} %fusion.2.places.refs_0_, bf16[2,64,1024]{2,1,0:T(8,128)(2,1)} %mine.1, bf16[2,64,1024]{2,1,0:T(8,128)(2,1)S(1)} %collective-permute-done.swapped, bf16[2,64,1024]{2,1,0:T(8,128)(2,1)S(1)} %collective-permute-done.2.back.refs_0_, ...), custom_call_target="tpu_custom_call" | custom-call | bytes 2097152 | tf_op jit(solution)/shard_map/pallas_call | solution.py:109
  16.6 2.0 %collective-permute-start.6 = (bf16[2,64,1024]{2,1,0:T(8,128)(2,1)S(1)}, bf16[2,64,1024]{2,1,0:T(8,128)(2,1)S(1)}, u32[]{:S(2)}, u32[]{:S(2)}) collective-permute-start(bf16[2,64,1024]{2,1,0:T(8,128)(2,1)S(1)} %shard_map.30), channel_id=1, source_target_pairs={{0,16},{1,17},{2,18},{3,19},{4,20},{5,21},{6,22},{7,23},{8,24},{9,... | collective-permute-start | bytes 786440 | tf_op jit(solution)/shard_map/ppermute | solution.py:25
  18.6 3.0 %collective-permute-start.8 = (bf16[2,64,1024]{2,1,0:T(8,128)(2,1)S(1)}, bf16[2,64,1024]{2,1,0:T(8,128)(2,1)S(1)}, u32[]{:S(2)}, u32[]{:S(2)}) collective-permute-start(bf16[2,64,1024]{2,1,0:T(8,128)(2,1)S(1)} %shard_map.30), channel_id=1, source_target_pairs={{0,32},{1,33},{2,34},{3,35},{4,36},{5,37},{6,38},{7,39},{8,40},{9,... | collective-permute-start | bytes 786440 | tf_op jit(solution)/shard_map/ppermute | solution.py:25
  21.6 0.6 shard_map.31.refs_1_.refs_3_
  22.4 1.5 %collective-permute-start.7 = (bf16[2,64,1024]{2,1,0:T(8,128)(2,1)S(1)}, bf16[2,64,1024]{2,1,0:T(8,128)(2,1)S(1)}, u32[]{:S(2)}, u32[]{:S(2)}) collective-permute-start(bf16[2,64,1024]{2,1,0:T(8,128)(2,1)S(1)} %shard_map.32), channel_id=1, source_target_pairs={{0,32},{1,33},{2,34},{3,35},{4,36},{5,37},{6,38},{7,39},{8,40},{9,... | collective-permute-start | bytes 786440 | tf_op jit(solution)/shard_map/ppermute | solution.py:25
  23.9 1.1 %collective-permute-done.8.refs_1_.refs_0_ = bf16[2,64,1024]{2,1,0:T(8,128)(2,1)S(1)} collective-permute-done((bf16[2,64,1024]{2,1,0:T(8,128)(2,1)S(1)}, bf16[2,64,1024]{2,1,0:T(8,128)(2,1)S(1)}, u32[]{:S(2)}, u32[]{:S(2)}) %collective-permute-start.8) | collective-permute-done | bytes 262176 | tf_op jit(solution)/shard_map/ppermute | solution.py:25
  25.0 0.6 shard_map.33.refs_1_.refs_3_
  25.6 1.5 %collective-permute-start.10 = (bf16[2,64,1024]{2,1,0:T(8,128)(2,1)S(1)}, bf16[2,64,1024]{2,1,0:T(8,128)(2,1)S(1)}, u32[]{:S(2)}, u32[]{:S(2)}) collective-permute-start(bf16[2,64,1024]{2,1,0:T(8,128)(2,1)S(1)} %shard_map.34), channel_id=1, source_target_pairs={{0,16},{1,17},{2,18},{3,19},{4,20},{5,21},{6,22},{7,23},{8,24},{9,... | collective-permute-start | bytes 786440 | tf_op jit(solution)/shard_map/ppermute | solution.py:25
  27.1 2.0 %collective-permute-start.17 = (bf16[4,2,64,1024]{3,2,1,0:T(8,128)(2,1)S(1)}, bf16[4,2,64,1024]{3,2,1,0:T(8,128)(2,1)S(1)}, u32[]{:S(2)}, u32[]{:S(2)}) collective-permute-start(bf16[4,2,64,1024]{3,2,1,0:T(8,128)(2,1)S(1)} %shard_map.28.refs_0_.left.ring), channel_id=1, source_target_pairs={{0,3},{1,0},{2,1},{3,2},{4,7},{5,4},{6,5},{7,6},{8,11},{9,8},{10,9... | collective-permute-start | bytes 3145736 | tf_op jit(solution)/shard_map/ppermute | solution.py:25
  29.1 1.3 %collective-permute-start.12 = (bf16[2,64,1024]{2,1,0:T(8,128)(2,1)S(1)}, bf16[2,64,1024]{2,1,0:T(8,128)(2,1)S(1)}, u32[]{:S(2)}, u32[]{:S(2)}) collective-permute-start(bf16[2,64,1024]{2,1,0:T(8,128)(2,1)S(1)} %shard_map.34), channel_id=1, source_target_pairs={{0,32},{1,33},{2,34},{3,35},{4,36},{5,37},{6,38},{7,39},{8,40},{9,... | collective-permute-start | bytes 786440 | tf_op jit(solution)/shard_map/ppermute | solution.py:25
  30.4 0.6 shard_map.35.refs_1_.refs_3_
  31.2 2.7 %collective-permute-start.11 = (bf16[2,64,1024]{2,1,0:T(8,128)(2,1)S(1)}, bf16[2,64,1024]{2,1,0:T(8,128)(2,1)S(1)}, u32[]{:S(2)}, u32[]{:S(2)}) collective-permute-start(bf16[2,64,1024]{2,1,0:T(8,128)(2,1)S(1)} %shard_map.36), channel_id=1, source_target_pairs={{0,32},{1,33},{2,34},{3,35},{4,36},{5,37},{6,38},{7,39},{8,40},{9,... | collective-permute-start | bytes 786440 | tf_op jit(solution)/shard_map/ppermute | solution.py:25
  33.9 0.7 %collective-permute-done.12.refs_1_.refs_0_ = bf16[2,64,1024]{2,1,0:T(8,128)(2,1)S(1)} collective-permute-done((bf16[2,64,1024]{2,1,0:T(8,128)(2,1)S(1)}, bf16[2,64,1024]{2,1,0:T(8,128)(2,1)S(1)}, u32[]{:S(2)}, u32[]{:S(2)}) %collective-permute-start.12) | collective-permute-done | bytes 262176 | tf_op jit(solution)/shard_map/ppermute | solution.py:25
  34.6 0.6 shard_map.37.refs_1_.refs_3_
  35.2 3.5 %collective-permute-start.14 = (bf16[2,64,1024]{2,1,0:T(8,128)(2,1)S(1)}, bf16[2,64,1024]{2,1,0:T(8,128)(2,1)S(1)}, u32[]{:S(2)}, u32[]{:S(2)}) collective-permute-start(bf16[2,64,1024]{2,1,0:T(8,128)(2,1)S(1)} %shard_map.38), channel_id=1, source_target_pairs={{0,16},{1,17},{2,18},{3,19},{4,20},{5,21},{6,22},{7,23},{8,24},{9,... | collective-permute-start | bytes 786440 | tf_op jit(solution)/shard_map/ppermute | solution.py:25
  38.7 1.2 %collective-permute-done.14.refs_2_ = bf16[2,64,1024]{2,1,0:T(8,128)(2,1)S(1)} collective-permute-done((bf16[2,64,1024]{2,1,0:T(8,128)(2,1)S(1)}, bf16[2,64,1024]{2,1,0:T(8,128)(2,1)S(1)}, u32[]{:S(2)}, u32[]{:S(2)}) %collective-permute-start.14) | collective-permute-done | bytes 262176 | tf_op jit(solution)/shard_map/ppermute | solution.py:25
  40.5 0.8 %collective-permute-start.15 = (bf16[2,64,1024]{2,1,0:T(8,128)(2,1)S(1)}, bf16[2,64,1024]{2,1,0:T(8,128)(2,1)S(1)}, u32[]{:S(2)}, u32[]{:S(2)}) collective-permute-start(bf16[2,64,1024]{2,1,0:T(8,128)(2,1)S(1)} %shard_map.40), channel_id=1, source_target_pairs={{0,16},{1,17},{2,18},{3,19},{4,20},{5,21},{6,22},{7,23},{8,24},{9,... | collective-permute-start | bytes 786440 | tf_op jit(solution)/shard_map/ppermute | solution.py:25
  41.6 1.0 %collective-permute-start.18 = (bf16[2,64,1024]{2,1,0:T(8,128)(2,1)S(1)}, bf16[2,64,1024]{2,1,0:T(8,128)(2,1)S(1)}, u32[]{:S(2)}, u32[]{:S(2)}) collective-permute-start(bf16[2,64,1024]{2,1,0:T(8,128)(2,1)S(1)} %shard_map.38), channel_id=1, source_target_pairs={{0,32},{1,33},{2,34},{3,35},{4,36},{5,37},{6,38},{7,39},{8,40},{9,... | collective-permute-start | bytes 786440 | tf_op jit(solution)/shard_map/ppermute | solution.py:25
  42.7 1.7 %collective-permute-start.21 = (bf16[2,2,64,1024]{3,2,1,0:T(8,128)(2,1)S(1)}, bf16[2,2,64,1024]{3,2,1,0:T(8,128)(2,1)S(1)}, u32[]{:S(2)}, u32[]{:S(2)}) collective-permute-start(bf16[2,2,64,1024]{3,2,1,0:T(8,128)(2,1)S(1)} %slice.9), channel_id=1, source_target_pairs={{0,3},{1,0},{2,1},{3,2},{4,7},{5,4},{6,5},{7,6},{8,11},{9,8},{10,9... | collective-permute-start | bytes 1572872 | tf_op jit(solution)/shard_map/ppermute | solution.py:25
  45.7 7.1 %shard_map.45.refs_1_.acc = f32[2,1024,1024]{2,1,0:T(8,128)S(1)} custom-call(bf16[4,2,4,64,1024]{4,3,2,1,0:T(8,128)(2,1)S(1)} %shard_map.41.right, bf16[1024,512]{1,0:T(8,128)(2,1)S(1)} %get-tuple-element.11.refs_0_, bf16[1024,512]{1,0:T(8,128)(2,1)S(1)} %get-tuple-element.12.refs_1_, bf16[1024,512]{1,0:T(8,128)(2,1)S(1)} %get-tuple-element.13.refs_2_, ...), custom_call_target="tpu_custom_call" | custom-call | flops 6442450944 | bytes 8388608 | tf_op jit(solution)/shard_map/pallas_call | solution.py:198
  52.9 2.1 %collective-permute-start.19 = (bf16[2,64,1024]{2,1,0:T(8,128)(2,1)S(1)}, bf16[2,64,1024]{2,1,0:T(8,128)(2,1)S(1)}, u32[]{:S(2)}, u32[]{:S(2)}) collective-permute-start(bf16[2,64,1024]{2,1,0:T(8,128)(2,1)S(1)} %shard_map.46.far_own), channel_id=1, source_target_pairs={{0,16},{1,17},{2,18},{3,19},{4,20},{5,21},{6,22},{7,23},{8,24},{9,... | collective-permute-start | bytes 786440 | tf_op jit(solution)/shard_map/ppermute | solution.py:25
  55.0 1.2 %collective-permute-done.19.far_swapped = bf16[2,64,1024]{2,1,0:T(8,128)(2,1)S(1)} collective-permute-done((bf16[2,64,1024]{2,1,0:T(8,128)(2,1)S(1)}, bf16[2,64,1024]{2,1,0:T(8,128)(2,1)S(1)}, u32[]{:S(2)}, u32[]{:S(2)}) %collective-permute-start.19) | collective-permute-done | bytes 262176 | tf_op jit(solution)/shard_map/ppermute | solution.py:25
  56.1 6.5 %shard_map.47 = f32[2,1024,1024]{2,1,0:T(8,128)} custom-call(s32[16]{0:T(128)S(1)} %fusion.2.places.refs_0_, f32[2,1024,1024]{2,1,0:T(8,128)S(1)} %shard_map.45.refs_1_.acc, bf16[4,2,4,64,1024]{4,3,2,1,0:T(8,128)(2,1)S(1)} %shard_map.41.right, bf16[2,64,1024]{2,1,0:T(8,128)(2,1)S(1)} %shard_map.46.far_own, ...), custom_call_target="tpu_custom_call" | custom-call | flops 3221225472 | bytes 9437184 | tf_op jit(solution)/shard_map/pallas_call | solution.py:241
  (36 shorter events, 2.8 us)
Async XLA Ops:
  0.0 11.6 %collective-permute-start = (bf16[2,64,1024]{2,1,0:T(8,128)(2,1)}, bf16[2,64,1024]{2,1,0:T(8,128)(2,1)S(1)}, u32[]{:S(2)}, u32[]{:S(2)}) collective-permute-start(bf16[2,64,1024]{2,1,0:T(8,128)(2,1)} %mine.1), channel_id=1, source_target_pairs={{0,16},{1,17},{2,18},{3,19},{4,20},{5,21},{6,22},{7,23},{8,24},{9,... | collective-permute-start | bytes 786440 | tf_op jit(solution)/shard_map/ppermute | solution.py:25
  3.2 9.2 %collective-permute-start.5 = (bf16[2,64,1024]{2,1,0:T(8,128)(2,1)}, bf16[2,64,1024]{2,1,0:T(8,128)(2,1)S(1)}, u32[]{:S(2)}, u32[]{:S(2)}) collective-permute-start(bf16[2,64,1024]{2,1,0:T(8,128)(2,1)} %bitcast.17), channel_id=1, source_target_pairs={{0,8},{1,9},{2,10},{3,11},{4,12},{5,13},{6,14},{7,15},{8,0},{9,1},... | collective-permute-start | bytes 786440 | tf_op jit(solution)/shard_map/ppermute | solution.py:25
  4.4 8.0 %collective-permute-start.4 = (bf16[2,64,1024]{2,1,0:T(8,128)(2,1)}, bf16[2,64,1024]{2,1,0:T(8,128)(2,1)S(1)}, u32[]{:S(2)}, u32[]{:S(2)}) collective-permute-start(bf16[2,64,1024]{2,1,0:T(8,128)(2,1)} %bitcast.18), channel_id=1, source_target_pairs={{0,12},{1,13},{2,14},{3,15},{4,0},{5,1},{6,2},{7,3},{8,4},{9,5},{1... | collective-permute-start | bytes 786440 | tf_op jit(solution)/shard_map/ppermute | solution.py:25
  5.2 8.1 %collective-permute-start.3 = (bf16[2,64,1024]{2,1,0:T(8,128)(2,1)}, bf16[2,64,1024]{2,1,0:T(8,128)(2,1)S(1)}, u32[]{:S(2)}, u32[]{:S(2)}) collective-permute-start(bf16[2,64,1024]{2,1,0:T(8,128)(2,1)} %bitcast.19), channel_id=1, source_target_pairs={{0,4},{1,5},{2,6},{3,7},{4,8},{5,9},{6,10},{7,11},{8,12},{9,13},{1... | collective-permute-start | bytes 786440 | tf_op jit(solution)/shard_map/ppermute | solution.py:25
  5.9 9.2 %collective-permute-start.2 = (bf16[2,64,1024]{2,1,0:T(8,128)(2,1)}, bf16[2,64,1024]{2,1,0:T(8,128)(2,1)S(1)}, u32[]{:S(2)}, u32[]{:S(2)}) collective-permute-start(bf16[2,64,1024]{2,1,0:T(8,128)(2,1)} %mine.1), channel_id=1, source_target_pairs={{0,32},{1,33},{2,34},{3,35},{4,36},{5,37},{6,38},{7,39},{8,40},{9,... | collective-permute-start | bytes 786440 | tf_op jit(solution)/shard_map/ppermute | solution.py:25
  11.6 10.0 %collective-permute-start.1 = (bf16[2,64,1024]{2,1,0:T(8,128)(2,1)S(1)}, bf16[2,64,1024]{2,1,0:T(8,128)(2,1)S(1)}, u32[]{:S(2)}, u32[]{:S(2)}) collective-permute-start(bf16[2,64,1024]{2,1,0:T(8,128)(2,1)S(1)} %collective-permute-done.swapped), channel_id=1, source_target_pairs={{0,32},{1,33},{2,34},{3,35},{4,36},{5,37},{6,38},{7,39},{8,40},{9,... | collective-permute-start | bytes 786440 | tf_op jit(solution)/shard_map/ppermute | solution.py:25
  16.6 5.0 %collective-permute-start.6 = (bf16[2,64,1024]{2,1,0:T(8,128)(2,1)S(1)}, bf16[2,64,1024]{2,1,0:T(8,128)(2,1)S(1)}, u32[]{:S(2)}, u32[]{:S(2)}) collective-permute-start(bf16[2,64,1024]{2,1,0:T(8,128)(2,1)S(1)} %shard_map.30), channel_id=1, source_target_pairs={{0,16},{1,17},{2,18},{3,19},{4,20},{5,21},{6,22},{7,23},{8,24},{9,... | collective-permute-start | bytes 786440 | tf_op jit(solution)/shard_map/ppermute | solution.py:25
  18.6 6.4 %collective-permute-start.8 = (bf16[2,64,1024]{2,1,0:T(8,128)(2,1)S(1)}, bf16[2,64,1024]{2,1,0:T(8,128)(2,1)S(1)}, u32[]{:S(2)}, u32[]{:S(2)}) collective-permute-start(bf16[2,64,1024]{2,1,0:T(8,128)(2,1)S(1)} %shard_map.30), channel_id=1, source_target_pairs={{0,32},{1,33},{2,34},{3,35},{4,36},{5,37},{6,38},{7,39},{8,40},{9,... | collective-permute-start | bytes 786440 | tf_op jit(solution)/shard_map/ppermute | solution.py:25
  22.3 2.7 %collective-permute-start.9 = (bf16[2,64,1024]{2,1,0:T(8,128)(2,1)S(1)}, bf16[2,64,1024]{2,1,0:T(8,128)(2,1)S(1)}, u32[]{:S(2)}, u32[]{:S(2)}) collective-permute-start(bf16[2,64,1024]{2,1,0:T(8,128)(2,1)S(1)} %shard_map.32), channel_id=1, source_target_pairs={{0,16},{1,17},{2,18},{3,19},{4,20},{5,21},{6,22},{7,23},{8,24},{9,... | collective-permute-start | bytes 786440 | tf_op jit(solution)/shard_map/ppermute | solution.py:25
  22.4 8.0 %collective-permute-start.7 = (bf16[2,64,1024]{2,1,0:T(8,128)(2,1)S(1)}, bf16[2,64,1024]{2,1,0:T(8,128)(2,1)S(1)}, u32[]{:S(2)}, u32[]{:S(2)}) collective-permute-start(bf16[2,64,1024]{2,1,0:T(8,128)(2,1)S(1)} %shard_map.32), channel_id=1, source_target_pairs={{0,32},{1,33},{2,34},{3,35},{4,36},{5,37},{6,38},{7,39},{8,40},{9,... | collective-permute-start | bytes 786440 | tf_op jit(solution)/shard_map/ppermute | solution.py:25
  25.6 4.8 %collective-permute-start.10 = (bf16[2,64,1024]{2,1,0:T(8,128)(2,1)S(1)}, bf16[2,64,1024]{2,1,0:T(8,128)(2,1)S(1)}, u32[]{:S(2)}, u32[]{:S(2)}) collective-permute-start(bf16[2,64,1024]{2,1,0:T(8,128)(2,1)S(1)} %shard_map.34), channel_id=1, source_target_pairs={{0,16},{1,17},{2,18},{3,19},{4,20},{5,21},{6,22},{7,23},{8,24},{9,... | collective-permute-start | bytes 786440 | tf_op jit(solution)/shard_map/ppermute | solution.py:25
  27.1 15.6 %collective-permute-start.17 = (bf16[4,2,64,1024]{3,2,1,0:T(8,128)(2,1)S(1)}, bf16[4,2,64,1024]{3,2,1,0:T(8,128)(2,1)S(1)}, u32[]{:S(2)}, u32[]{:S(2)}) collective-permute-start(bf16[4,2,64,1024]{3,2,1,0:T(8,128)(2,1)S(1)} %shard_map.28.refs_0_.left.ring), channel_id=1, source_target_pairs={{0,3},{1,0},{2,1},{3,2},{4,7},{5,4},{6,5},{7,6},{8,11},{9,8},{10,9... | collective-permute-start | bytes 3145736 | tf_op jit(solution)/shard_map/ppermute | solution.py:25
  29.1 15.3 %collective-permute-start.16 = (bf16[4,2,64,1024]{3,2,1,0:T(8,128)(2,1)S(1)}, bf16[4,2,64,1024]{3,2,1,0:T(8,128)(2,1)S(1)}, u32[]{:S(2)}, u32[]{:S(2)}) collective-permute-start(bf16[4,2,64,1024]{3,2,1,0:T(8,128)(2,1)S(1)} %shard_map.28.refs_0_.left.ring), channel_id=1, source_target_pairs={{0,1},{1,2},{2,3},{3,0},{4,5},{5,6},{6,7},{7,4},{8,9},{9,10},{10,1... | collective-permute-start | bytes 3145736 | tf_op jit(solution)/shard_map/ppermute | solution.py:25
  29.1 5.5 %collective-permute-start.12 = (bf16[2,64,1024]{2,1,0:T(8,128)(2,1)S(1)}, bf16[2,64,1024]{2,1,0:T(8,128)(2,1)S(1)}, u32[]{:S(2)}, u32[]{:S(2)}) collective-permute-start(bf16[2,64,1024]{2,1,0:T(8,128)(2,1)S(1)} %shard_map.34), channel_id=1, source_target_pairs={{0,32},{1,33},{2,34},{3,35},{4,36},{5,37},{6,38},{7,39},{8,40},{9,... | collective-permute-start | bytes 786440 | tf_op jit(solution)/shard_map/ppermute | solution.py:25
  31.0 3.6 %collective-permute-start.13 = (bf16[2,64,1024]{2,1,0:T(8,128)(2,1)S(1)}, bf16[2,64,1024]{2,1,0:T(8,128)(2,1)S(1)}, u32[]{:S(2)}, u32[]{:S(2)}) collective-permute-start(bf16[2,64,1024]{2,1,0:T(8,128)(2,1)S(1)} %shard_map.36), channel_id=1, source_target_pairs={{0,16},{1,17},{2,18},{3,19},{4,20},{5,21},{6,22},{7,23},{8,24},{9,... | collective-permute-start | bytes 786440 | tf_op jit(solution)/shard_map/ppermute | solution.py:25
  31.2 7.5 %collective-permute-start.11 = (bf16[2,64,1024]{2,1,0:T(8,128)(2,1)S(1)}, bf16[2,64,1024]{2,1,0:T(8,128)(2,1)S(1)}, u32[]{:S(2)}, u32[]{:S(2)}) collective-permute-start(bf16[2,64,1024]{2,1,0:T(8,128)(2,1)S(1)} %shard_map.36), channel_id=1, source_target_pairs={{0,32},{1,33},{2,34},{3,35},{4,36},{5,37},{6,38},{7,39},{8,40},{9,... | collective-permute-start | bytes 786440 | tf_op jit(solution)/shard_map/ppermute | solution.py:25
  35.2 4.6 %collective-permute-start.14 = (bf16[2,64,1024]{2,1,0:T(8,128)(2,1)S(1)}, bf16[2,64,1024]{2,1,0:T(8,128)(2,1)S(1)}, u32[]{:S(2)}, u32[]{:S(2)}) collective-permute-start(bf16[2,64,1024]{2,1,0:T(8,128)(2,1)S(1)} %shard_map.38), channel_id=1, source_target_pairs={{0,16},{1,17},{2,18},{3,19},{4,20},{5,21},{6,22},{7,23},{8,24},{9,... | collective-permute-start | bytes 786440 | tf_op jit(solution)/shard_map/ppermute | solution.py:25
  40.5 4.7 %collective-permute-start.15 = (bf16[2,64,1024]{2,1,0:T(8,128)(2,1)S(1)}, bf16[2,64,1024]{2,1,0:T(8,128)(2,1)S(1)}, u32[]{:S(2)}, u32[]{:S(2)}) collective-permute-start(bf16[2,64,1024]{2,1,0:T(8,128)(2,1)S(1)} %shard_map.40), channel_id=1, source_target_pairs={{0,16},{1,17},{2,18},{3,19},{4,20},{5,21},{6,22},{7,23},{8,24},{9,... | collective-permute-start | bytes 786440 | tf_op jit(solution)/shard_map/ppermute | solution.py:25
  41.6 11.2 %collective-permute-start.18 = (bf16[2,64,1024]{2,1,0:T(8,128)(2,1)S(1)}, bf16[2,64,1024]{2,1,0:T(8,128)(2,1)S(1)}, u32[]{:S(2)}, u32[]{:S(2)}) collective-permute-start(bf16[2,64,1024]{2,1,0:T(8,128)(2,1)S(1)} %shard_map.38), channel_id=1, source_target_pairs={{0,32},{1,33},{2,34},{3,35},{4,36},{5,37},{6,38},{7,39},{8,40},{9,... | collective-permute-start | bytes 786440 | tf_op jit(solution)/shard_map/ppermute | solution.py:25
  42.7 12.3 %collective-permute-start.21 = (bf16[2,2,64,1024]{3,2,1,0:T(8,128)(2,1)S(1)}, bf16[2,2,64,1024]{3,2,1,0:T(8,128)(2,1)S(1)}, u32[]{:S(2)}, u32[]{:S(2)}) collective-permute-start(bf16[2,2,64,1024]{3,2,1,0:T(8,128)(2,1)S(1)} %slice.9), channel_id=1, source_target_pairs={{0,3},{1,0},{2,1},{3,2},{4,7},{5,4},{6,5},{7,6},{8,11},{9,8},{10,9... | collective-permute-start | bytes 1572872 | tf_op jit(solution)/shard_map/ppermute | solution.py:25
  44.4 10.6 %collective-permute-start.20 = (bf16[2,2,64,1024]{3,2,1,0:T(8,128)(2,1)S(1)}, bf16[2,2,64,1024]{3,2,1,0:T(8,128)(2,1)S(1)}, u32[]{:S(2)}, u32[]{:S(2)}) collective-permute-start(bf16[2,2,64,1024]{3,2,1,0:T(8,128)(2,1)S(1)} %slice.8), channel_id=1, source_target_pairs={{0,1},{1,2},{2,3},{3,0},{4,5},{5,6},{6,7},{7,4},{8,9},{9,10},{10,1... | collective-permute-start | bytes 1572872 | tf_op jit(solution)/shard_map/ppermute | solution.py:25
  52.9 3.2 %collective-permute-start.19 = (bf16[2,64,1024]{2,1,0:T(8,128)(2,1)S(1)}, bf16[2,64,1024]{2,1,0:T(8,128)(2,1)S(1)}, u32[]{:S(2)}, u32[]{:S(2)}) collective-permute-start(bf16[2,64,1024]{2,1,0:T(8,128)(2,1)S(1)} %shard_map.46.far_own), channel_id=1, source_target_pairs={{0,16},{1,17},{2,18},{3,19},{4,20},{5,21},{6,22},{7,23},{8,24},{9,... | collective-permute-start | bytes 786440 | tf_op jit(solution)/shard_map/ppermute | solution.py:25

commit v3 on v2

--- a/solution.py
+++ b/solution.py
@@ -284,6 +284,7 @@
     far_back = permute(back[:2], second_axis(1))
     far_ahead = permute(ahead[2:], second_axis(-1))
 
+    sides = []
     held = [right_panel, swapped]
     waiting = []
     for slot in range(2, FAR, 2):
@@ -295,14 +296,17 @@
             due = waiting[:1] if slot < 12 else waiting[:1]
             waiting = waiting[1:]
             right = place(right, [slot] + [s for s, _ in due], [part] + [p for _, p in due], places)
-        part, = after((part,), right)
+        others = {10: (back, ahead), 12: [s for side in sides for s in side]}.get(slot, ())
+        if slot == 10:
+            sides = [turn(group) for group in (ring, back, ahead)]
+        part, = after((part,), right, *others)
         held[shard] = part
         waiting.append((slot + 1, permute(part, other_core)))
     far = permute(held[0], along_z(1))
     right = place(right, [s for s, _ in waiting], [p for _, p in waiting], places)
 
     groups = (ring, back, ahead)
-    acc = early(right, [side for group in groups for side in turn(group)])
+    acc = early(right, [s for side in sides for s in side])
     far, = after((far,), acc)
     return late(places, acc, right, (far, permute(far, other_core)), groups, far_back, far_ahead)
 

time: 62.7 us -> 60.9 us (0.971)
  starting transfers between devices: 35.6 us -> 34.3 us
  waiting for transfers between devices: 5.84 us -> 5.18 us
    ppermute x22, starting transfers between devices: 35.6 us -> 34.3 us  [permute(): return lax.ppermute(value, AXES, pairs)]
    ppermute x22, waiting for transfers between devices: 5.84 us -> 5.18 us  [permute(): return lax.ppermute(value, AXES, pairs)]
  transfers between devices with their start and end apart: 22 -> 22, of which waited for: 6 -> 6; matrix products, arithmetic and copies ran while one was open for 0% -> 0% of each run, Pallas kernels for 23% -> 22%
where the time goes in v3:
time: 60.9 us; the launch traced here: 60.7 us
  starting transfers between devices  34.3 us (56%)
  Pallas kernels  20.7 us (34%)
  waiting for transfers between devices  5.18 us (9%)
    ppermute x22, starting transfers between devices, permute(): return lax.ppermute(value, AXES, pairs)  34.3 us
    pallas_call x1, Pallas kernels, early(): pl.pallas_call(early_kernel, out_shape=pltpu.VMEM((2, 1024, 1024), jnp.fl...  7.14 us
    pallas_call x1, Pallas kernels, late(): pl.pallas_call(late_kernel, grid=(4,), out_shape=jax.ShapeDtypeStruct((2,...  6.48 us
    ppermute x22, waiting for transfers between devices, permute(): return lax.ppermute(value, AXES, pairs)  5.18 us
    pallas_call x6, Pallas kernels, place(): pl.pallas_call(lambda *refs: place_kernel(slots, *refs), out_shape=RIGHT,...  3.66 us
    pallas_call x1, Pallas kernels, first(): pl.pallas_call(first_kernel, out_shape=RIGHT, in_specs=[SMEM, HBM] + [VME...  1.51 us
  transfers between devices with their start and end apart: 22, of which 6 were waited for; matrix products, arithmetic and copies ran while one was open for 0% of the time, Pallas kernels for 22%

profile of v3, /device:TPU:1, one launch (start us, length us, event | category | flops | bytes accessed | tf_op | source)
XLA Modules:
  0.0 60.7 jit_solution(746885827855955758)
XLA Ops:
  0.0 3.2 %collective-permute-start = (bf16[2,64,1024]{2,1,0:T(8,128)(2,1)}, bf16[2,64,1024]{2,1,0:T(8,128)(2,1)S(1)}, u32[]{:S(2)}, u32[]{:S(2)}) collective-permute-start(bf16[2,64,1024]{2,1,0:T(8,128)(2,1)} %mine.1), channel_id=1, source_target_pairs={{0,16},{1,17},{2,18},{3,19},{4,20},{5,21},{6,22},{7,23},{8,24},{9,... | collective-permute-start | bytes 786440 | tf_op jit(solution)/shard_map/ppermute | solution.py:25
  3.2 1.2 %collective-permute-start.5 = (bf16[2,64,1024]{2,1,0:T(8,128)(2,1)}, bf16[2,64,1024]{2,1,0:T(8,128)(2,1)S(1)}, u32[]{:S(2)}, u32[]{:S(2)}) collective-permute-start(bf16[2,64,1024]{2,1,0:T(8,128)(2,1)} %bitcast.17), channel_id=1, source_target_pairs={{0,8},{1,9},{2,10},{3,11},{4,12},{5,13},{6,14},{7,15},{8,0},{9,1},... | collective-permute-start | bytes 786440 | tf_op jit(solution)/shard_map/ppermute | solution.py:25
  4.4 0.8 %collective-permute-start.4 = (bf16[2,64,1024]{2,1,0:T(8,128)(2,1)}, bf16[2,64,1024]{2,1,0:T(8,128)(2,1)S(1)}, u32[]{:S(2)}, u32[]{:S(2)}) collective-permute-start(bf16[2,64,1024]{2,1,0:T(8,128)(2,1)} %bitcast.18), channel_id=1, source_target_pairs={{0,12},{1,13},{2,14},{3,15},{4,0},{5,1},{6,2},{7,3},{8,4},{9,5},{1... | collective-permute-start | bytes 786440 | tf_op jit(solution)/shard_map/ppermute | solution.py:25
  5.2 0.7 %collective-permute-start.3 = (bf16[2,64,1024]{2,1,0:T(8,128)(2,1)}, bf16[2,64,1024]{2,1,0:T(8,128)(2,1)S(1)}, u32[]{:S(2)}, u32[]{:S(2)}) collective-permute-start(bf16[2,64,1024]{2,1,0:T(8,128)(2,1)} %bitcast.19), channel_id=1, source_target_pairs={{0,4},{1,5},{2,6},{3,7},{4,8},{5,9},{6,10},{7,11},{8,12},{9,13},{1... | collective-permute-start | bytes 786440 | tf_op jit(solution)/shard_map/ppermute | solution.py:25
  5.9 5.6 %collective-permute-start.2 = (bf16[2,64,1024]{2,1,0:T(8,128)(2,1)}, bf16[2,64,1024]{2,1,0:T(8,128)(2,1)S(1)}, u32[]{:S(2)}, u32[]{:S(2)}) collective-permute-start(bf16[2,64,1024]{2,1,0:T(8,128)(2,1)} %mine.1), channel_id=1, source_target_pairs={{0,32},{1,33},{2,34},{3,35},{4,36},{5,37},{6,38},{7,39},{8,40},{9,... | collective-permute-start | bytes 786440 | tf_op jit(solution)/shard_map/ppermute | solution.py:25
  11.6 0.8 %collective-permute-start.1 = (bf16[2,64,1024]{2,1,0:T(8,128)(2,1)S(1)}, bf16[2,64,1024]{2,1,0:T(8,128)(2,1)S(1)}, u32[]{:S(2)}, u32[]{:S(2)}) collective-permute-start(bf16[2,64,1024]{2,1,0:T(8,128)(2,1)S(1)} %collective-permute-done.swapped), channel_id=1, source_target_pairs={{0,32},{1,33},{2,34},{3,35},{4,36},{5,37},{6,38},{7,39},{8,40},{9,... | collective-permute-start | bytes 786440 | tf_op jit(solution)/shard_map/ppermute | solution.py:25
  12.4 0.9 %collective-permute-done.3.refs_0_ = bf16[2,64,1024]{2,1,0:T(8,128)(2,1)S(1)} collective-permute-done((bf16[2,64,1024]{2,1,0:T(8,128)(2,1)}, bf16[2,64,1024]{2,1,0:T(8,128)(2,1)S(1)}, u32[]{:S(2)}, u32[]{:S(2)}) %collective-permute-start.3) | collective-permute-done | bytes 262176 | tf_op jit(solution)/shard_map/ppermute | solution.py:25
  13.3 1.0 %shard_map.28.refs_0_.left.ring = bf16[4,2,64,1024]{3,2,1,0:T(8,128)(2,1)S(1)} custom-call(bf16[2,64,1024]{2,1,0:T(8,128)(2,1)} %bitcast.20, bf16[2,64,1024]{2,1,0:T(8,128)(2,1)S(1)} %collective-permute-done.3.refs_0_, bf16[2,64,1024]{2,1,0:T(8,128)(2,1)S(1)} %collective-permute-done.4.refs_1_, bf16[2,64,1024]{2,1,0:T(8,128)(2,1)S(1)} %collective-permute-done.5.refs_2_), custom_call_target="tpu_custom_call" | custom-call | bytes 2097152 | tf_op jit(solution)/shard_map/pallas_call | solution.py:86
  14.2 0.8 %collective-permute-done.2.back.refs_0_ = bf16[2,64,1024]{2,1,0:T(8,128)(2,1)S(1)} collective-permute-done((bf16[2,64,1024]{2,1,0:T(8,128)(2,1)}, bf16[2,64,1024]{2,1,0:T(8,128)(2,1)S(1)}, u32[]{:S(2)}, u32[]{:S(2)}) %collective-permute-start.2) | collective-permute-done | bytes 262176 | tf_op jit(solution)/shard_map/ppermute | solution.py:25
  15.1 1.5 %shard_map.29.refs_1_.refs_3_ = bf16[4,2,4,64,1024]{4,3,2,1,0:T(8,128)(2,1)S(1)} custom-call(s32[16]{0:T(128)S(1)} %fusion.2.places.refs_0_, bf16[2,64,1024]{2,1,0:T(8,128)(2,1)} %mine.1, bf16[2,64,1024]{2,1,0:T(8,128)(2,1)S(1)} %collective-permute-done.swapped, bf16[2,64,1024]{2,1,0:T(8,128)(2,1)S(1)} %collective-permute-done.2.back.refs_0_, ...), custom_call_target="tpu_custom_call" | custom-call | bytes 2097152 | tf_op jit(solution)/shard_map/pallas_call | solution.py:109
  16.6 2.0 %collective-permute-start.6 = (bf16[2,64,1024]{2,1,0:T(8,128)(2,1)S(1)}, bf16[2,64,1024]{2,1,0:T(8,128)(2,1)S(1)}, u32[]{:S(2)}, u32[]{:S(2)}) collective-permute-start(bf16[2,64,1024]{2,1,0:T(8,128)(2,1)S(1)} %shard_map.30), channel_id=1, source_target_pairs={{0,16},{1,17},{2,18},{3,19},{4,20},{5,21},{6,22},{7,23},{8,24},{9,... | collective-permute-start | bytes 786440 | tf_op jit(solution)/shard_map/ppermute | solution.py:25
  18.6 2.1 %collective-permute-start.15 = (bf16[4,2,64,1024]{3,2,1,0:T(8,128)(2,1)S(1)}, bf16[4,2,64,1024]{3,2,1,0:T(8,128)(2,1)S(1)}, u32[]{:S(2)}, u32[]{:S(2)}) collective-permute-start(bf16[4,2,64,1024]{3,2,1,0:T(8,128)(2,1)S(1)} %shard_map.28.refs_0_.left.ring), channel_id=1, source_target_pairs={{0,3},{1,0},{2,1},{3,2},{4,7},{5,4},{6,5},{7,6},{8,11},{9,8},{10,9... | collective-permute-start | bytes 3145736 | tf_op jit(solution)/shard_map/ppermute | solution.py:25
  20.7 2.4 %collective-permute-start.8 = (bf16[2,64,1024]{2,1,0:T(8,128)(2,1)S(1)}, bf16[2,64,1024]{2,1,0:T(8,128)(2,1)S(1)}, u32[]{:S(2)}, u32[]{:S(2)}) collective-permute-start(bf16[2,64,1024]{2,1,0:T(8,128)(2,1)S(1)} %shard_map.30), channel_id=1, source_target_pairs={{0,32},{1,33},{2,34},{3,35},{4,36},{5,37},{6,38},{7,39},{8,40},{9,... | collective-permute-start | bytes 786440 | tf_op jit(solution)/shard_map/ppermute | solution.py:25
  23.1 0.6 %shard_map.31.refs_1_.refs_3_ = bf16[4,2,4,64,1024]{4,3,2,1,0:T(8,128)(2,1)S(1)} custom-call(s32[16]{0:T(128)S(1)} %fusion.2.places.refs_0_, bf16[2,64,1024]{2,1,0:T(8,128)(2,1)S(1)} %collective-permute-done.1.refs_1_.refs_0_, bf16[2,64,1024]{2,1,0:T(8,128)(2,1)S(1)} %collective-permute-done.6.refs_2_, ...), custom_call_target="tpu_custom_call", output_to_operand_aliasing={{}: (3, {})} | custom-call | bytes 524288 | tf_op jit(solution)/shard_map/pallas_call | solution.py:147
  23.8 1.6 %collective-permute-start.7 = (bf16[2,64,1024]{2,1,0:T(8,128)(2,1)S(1)}, bf16[2,64,1024]{2,1,0:T(8,128)(2,1)S(1)}, u32[]{:S(2)}, u32[]{:S(2)}) collective-permute-start(bf16[2,64,1024]{2,1,0:T(8,128)(2,1)S(1)} %shard_map.32), channel_id=1, source_target_pairs={{0,32},{1,33},{2,34},{3,35},{4,36},{5,37},{6,38},{7,39},{8,40},{9,... | collective-permute-start | bytes 786440 | tf_op jit(solution)/shard_map/ppermute | solution.py:25
  25.5 0.9 %collective-permute-done.8.refs_1_.refs_0_ = bf16[2,64,1024]{2,1,0:T(8,128)(2,1)S(1)} collective-permute-done((bf16[2,64,1024]{2,1,0:T(8,128)(2,1)S(1)}, bf16[2,64,1024]{2,1,0:T(8,128)(2,1)S(1)}, u32[]{:S(2)}, u32[]{:S(2)}) %collective-permute-start.8) | collective-permute-done | bytes 262176 | tf_op jit(solution)/shard_map/ppermute | solution.py:25
  26.4 0.6 %shard_map.33.refs_1_.refs_3_ = bf16[4,2,4,64,1024]{4,3,2,1,0:T(8,128)(2,1)S(1)} custom-call(s32[16]{0:T(128)S(1)} %fusion.2.places.refs_0_, bf16[2,64,1024]{2,1,0:T(8,128)(2,1)S(1)} %collective-permute-done.8.refs_1_.refs_0_, bf16[2,64,1024]{2,1,0:T(8,128)(2,1)S(1)} %collective-permute-done.9.refs_2_, ...), custom_call_target="tpu_custom_call", output_to_operand_aliasing={{}: (3, {})} | custom-call | bytes 524288 | tf_op jit(solution)/shard_map/pallas_call | solution.py:147
  27.1 3.0 %collective-permute-start.10 = (bf16[2,64,1024]{2,1,0:T(8,128)(2,1)S(1)}, bf16[2,64,1024]{2,1,0:T(8,128)(2,1)S(1)}, u32[]{:S(2)}, u32[]{:S(2)}) collective-permute-start(bf16[2,64,1024]{2,1,0:T(8,128)(2,1)S(1)} %shard_map.34), channel_id=1, source_target_pairs={{0,16},{1,17},{2,18},{3,19},{4,20},{5,21},{6,22},{7,23},{8,24},{9,... | collective-permute-start | bytes 786440 | tf_op jit(solution)/shard_map/ppermute | solution.py:25
  30.1 1.7 %collective-permute-start.12 = (bf16[2,64,1024]{2,1,0:T(8,128)(2,1)S(1)}, bf16[2,64,1024]{2,1,0:T(8,128)(2,1)S(1)}, u32[]{:S(2)}, u32[]{:S(2)}) collective-permute-start(bf16[2,64,1024]{2,1,0:T(8,128)(2,1)S(1)} %shard_map.34), channel_id=1, source_target_pairs={{0,32},{1,33},{2,34},{3,35},{4,36},{5,37},{6,38},{7,39},{8,40},{9,... | collective-permute-start | bytes 786440 | tf_op jit(solution)/shard_map/ppermute | solution.py:25
  31.8 0.6 %shard_map.35.refs_1_.refs_3_ = bf16[4,2,4,64,1024]{4,3,2,1,0:T(8,128)(2,1)S(1)} custom-call(s32[16]{0:T(128)S(1)} %fusion.2.places.refs_0_, bf16[2,64,1024]{2,1,0:T(8,128)(2,1)S(1)} %collective-permute-done.7.refs_1_.refs_0_, bf16[2,64,1024]{2,1,0:T(8,128)(2,1)S(1)} %collective-permute-done.10.refs_2_, ...), custom_call_target="tpu_custom_call", output_to_operand_aliasing={{}: (3, {})} | custom-call | bytes 524288 | tf_op jit(solution)/shard_map/pallas_call | solution.py:147
  32.9 1.7 %collective-permute-start.11 = (bf16[2,64,1024]{2,1,0:T(8,128)(2,1)S(1)}, bf16[2,64,1024]{2,1,0:T(8,128)(2,1)S(1)}, u32[]{:S(2)}, u32[]{:S(2)}) collective-permute-start(bf16[2,64,1024]{2,1,0:T(8,128)(2,1)S(1)} %shard_map.36), channel_id=1, source_target_pairs={{0,32},{1,33},{2,34},{3,35},{4,36},{5,37},{6,38},{7,39},{8,40},{9,... | collective-permute-start | bytes 786440 | tf_op jit(solution)/shard_map/ppermute | solution.py:25
  34.7 1.0 %collective-permute-done.12.refs_1_.refs_0_ = bf16[2,64,1024]{2,1,0:T(8,128)(2,1)S(1)} collective-permute-done((bf16[2,64,1024]{2,1,0:T(8,128)(2,1)S(1)}, bf16[2,64,1024]{2,1,0:T(8,128)(2,1)S(1)}, u32[]{:S(2)}, u32[]{:S(2)}) %collective-permute-start.12) | collective-permute-done | bytes 262176 | tf_op jit(solution)/shard_map/ppermute | solution.py:25
  35.6 0.6 %shard_map.37.refs_1_.refs_3_ = bf16[4,2,4,64,1024]{4,3,2,1,0:T(8,128)(2,1)S(1)} custom-call(s32[16]{0:T(128)S(1)} %fusion.2.places.refs_0_, bf16[2,64,1024]{2,1,0:T(8,128)(2,1)S(1)} %collective-permute-done.12.refs_1_.refs_0_, bf16[2,64,1024]{2,1,0:T(8,128)(2,1)S(1)} %collective-permute-done.13.refs_2_, ...), custom_call_target="tpu_custom_call", output_to_operand_aliasing={{}: (3, {})} | custom-call | bytes 524288 | tf_op jit(solution)/shard_map/pallas_call | solution.py:147
  36.3 2.4 %collective-permute-start.16 = (bf16[2,64,1024]{2,1,0:T(8,128)(2,1)S(1)}, bf16[2,64,1024]{2,1,0:T(8,128)(2,1)S(1)}, u32[]{:S(2)}, u32[]{:S(2)}) collective-permute-start(bf16[2,64,1024]{2,1,0:T(8,128)(2,1)S(1)} %shard_map.38), channel_id=1, source_target_pairs={{0,16},{1,17},{2,18},{3,19},{4,20},{5,21},{6,22},{7,23},{8,24},{9,... | collective-permute-start | bytes 786440 | tf_op jit(solution)/shard_map/ppermute | solution.py:25
  39.9 0.6 %shard_map.39.refs_1_.refs_2_ = bf16[4,2,4,64,1024]{4,3,2,1,0:T(8,128)(2,1)S(1)} custom-call(s32[16]{0:T(128)S(1)} %fusion.2.places.refs_0_, bf16[2,64,1024]{2,1,0:T(8,128)(2,1)S(1)} %collective-permute-done.11.refs_1_.refs_0_, bf16[2,64,1024]{2,1,0:T(8,128)(2,1)S(1)} %collective-permute-done.16.refs_2_, ...), custom_call_target="tpu_custom_call", output_to_operand_aliasing={{}: (3, {})} | custom-call | bytes 524288 | tf_op jit(solution)/shard_map/pallas_call | solution.py:147
  40.5 0.9 %collective-permute-start.17 = (bf16[2,64,1024]{2,1,0:T(8,128)(2,1)S(1)}, bf16[2,64,1024]{2,1,0:T(8,128)(2,1)S(1)}, u32[]{:S(2)}, u32[]{:S(2)}) collective-permute-start(bf16[2,64,1024]{2,1,0:T(8,128)(2,1)S(1)} %shard_map.43), channel_id=1, source_target_pairs={{0,16},{1,17},{2,18},{3,19},{4,20},{5,21},{6,22},{7,23},{8,24},{9,... | collective-permute-start | bytes 786440 | tf_op jit(solution)/shard_map/ppermute | solution.py:25
  41.4 1.6 %collective-permute-start.18 = (bf16[2,64,1024]{2,1,0:T(8,128)(2,1)S(1)}, bf16[2,64,1024]{2,1,0:T(8,128)(2,1)S(1)}, u32[]{:S(2)}, u32[]{:S(2)}) collective-permute-start(bf16[2,64,1024]{2,1,0:T(8,128)(2,1)S(1)} %shard_map.38), channel_id=1, source_target_pairs={{0,32},{1,33},{2,34},{3,35},{4,36},{5,37},{6,38},{7,39},{8,40},{9,... | collective-permute-start | bytes 786440 | tf_op jit(solution)/shard_map/ppermute | solution.py:25
  43.0 1.5 %collective-permute-start.21 = (bf16[2,2,64,1024]{3,2,1,0:T(8,128)(2,1)S(1)}, bf16[2,2,64,1024]{3,2,1,0:T(8,128)(2,1)S(1)}, u32[]{:S(2)}, u32[]{:S(2)}) collective-permute-start(bf16[2,2,64,1024]{3,2,1,0:T(8,128)(2,1)S(1)} %slice.9), channel_id=1, source_target_pairs={{0,3},{1,0},{2,1},{3,2},{4,7},{5,4},{6,5},{7,6},{8,11},{9,8},{10,9... | collective-permute-start | bytes 1572872 | tf_op jit(solution)/shard_map/ppermute | solution.py:25
  44.7 0.6 shard_map.44.right
  45.3 7.1 %shard_map.45.refs_1_.acc = f32[2,1024,1024]{2,1,0:T(8,128)S(1)} custom-call(bf16[4,2,4,64,1024]{4,3,2,1,0:T(8,128)(2,1)S(1)} %shard_map.44.right, bf16[1024,512]{1,0:T(8,128)(2,1)S(1)} %get-tuple-element.11.refs_2_.refs_0_, bf16[1024,512]{1,0:T(8,128)(2,1)S(1)} %get-tuple-element.12.refs_3_.refs_1_, ...), custom_call_target="tpu_custom_call" | custom-call | flops 6442450944 | bytes 8388608 | tf_op jit(solution)/shard_map/pallas_call | solution.py:198
  52.8 1.4 %collective-permute-done.20.up = bf16[2,2,64,1024]{3,2,1,0:T(8,128)(2,1)S(1)} collective-permute-done((bf16[2,2,64,1024]{3,2,1,0:T(8,128)(2,1)S(1)}, bf16[2,2,64,1024]{3,2,1,0:T(8,128)(2,1)S(1)}, u32[]{:S(2)}, u32[]{:S(2)}) %collective-permute-start.20) | collective-permute-done | bytes 524320 | tf_op jit(solution)/shard_map/ppermute | solution.py:25
  54.2 6.5 %shard_map.47 = f32[2,1024,1024]{2,1,0:T(8,128)} custom-call(s32[16]{0:T(128)S(1)} %fusion.2.places.refs_0_, f32[2,1024,1024]{2,1,0:T(8,128)S(1)} %shard_map.45.refs_1_.acc, bf16[4,2,4,64,1024]{4,3,2,1,0:T(8,128)(2,1)S(1)} %shard_map.44.right, bf16[2,64,1024]{2,1,0:T(8,128)(2,1)S(1)} %shard_map.46.far_own, ...), custom_call_target="tpu_custom_call" | custom-call | flops 3221225472 | bytes 9437184 | tf_op jit(solution)/shard_map/pallas_call | solution.py:241
  (36 shorter events, 2.4 us)
Async XLA Ops:
  0.0 11.6 %collective-permute-start = (bf16[2,64,1024]{2,1,0:T(8,128)(2,1)}, bf16[2,64,1024]{2,1,0:T(8,128)(2,1)S(1)}, u32[]{:S(2)}, u32[]{:S(2)}) collective-permute-start(bf16[2,64,1024]{2,1,0:T(8,128)(2,1)} %mine.1), channel_id=1, source_target_pairs={{0,16},{1,17},{2,18},{3,19},{4,20},{5,21},{6,22},{7,23},{8,24},{9,... | collective-permute-start | bytes 786440 | tf_op jit(solution)/shard_map/ppermute | solution.py:25
  3.2 9.2 %collective-permute-start.5 = (bf16[2,64,1024]{2,1,0:T(8,128)(2,1)}, bf16[2,64,1024]{2,1,0:T(8,128)(2,1)S(1)}, u32[]{:S(2)}, u32[]{:S(2)}) collective-permute-start(bf16[2,64,1024]{2,1,0:T(8,128)(2,1)} %bitcast.17), channel_id=1, source_target_pairs={{0,8},{1,9},{2,10},{3,11},{4,12},{5,13},{6,14},{7,15},{8,0},{9,1},... | collective-permute-start | bytes 786440 | tf_op jit(solution)/shard_map/ppermute | solution.py:25
  4.4 8.0 %collective-permute-start.4 = (bf16[2,64,1024]{2,1,0:T(8,128)(2,1)}, bf16[2,64,1024]{2,1,0:T(8,128)(2,1)S(1)}, u32[]{:S(2)}, u32[]{:S(2)}) collective-permute-start(bf16[2,64,1024]{2,1,0:T(8,128)(2,1)} %bitcast.18), channel_id=1, source_target_pairs={{0,12},{1,13},{2,14},{3,15},{4,0},{5,1},{6,2},{7,3},{8,4},{9,5},{1... | collective-permute-start | bytes 786440 | tf_op jit(solution)/shard_map/ppermute | solution.py:25
  5.2 8.1 %collective-permute-start.3 = (bf16[2,64,1024]{2,1,0:T(8,128)(2,1)}, bf16[2,64,1024]{2,1,0:T(8,128)(2,1)S(1)}, u32[]{:S(2)}, u32[]{:S(2)}) collective-permute-start(bf16[2,64,1024]{2,1,0:T(8,128)(2,1)} %bitcast.19), channel_id=1, source_target_pairs={{0,4},{1,5},{2,6},{3,7},{4,8},{5,9},{6,10},{7,11},{8,12},{9,13},{1... | collective-permute-start | bytes 786440 | tf_op jit(solution)/shard_map/ppermute | solution.py:25
  5.9 9.2 %collective-permute-start.2 = (bf16[2,64,1024]{2,1,0:T(8,128)(2,1)}, bf16[2,64,1024]{2,1,0:T(8,128)(2,1)S(1)}, u32[]{:S(2)}, u32[]{:S(2)}) collective-permute-start(bf16[2,64,1024]{2,1,0:T(8,128)(2,1)} %mine.1), channel_id=1, source_target_pairs={{0,32},{1,33},{2,34},{3,35},{4,36},{5,37},{6,38},{7,39},{8,40},{9,... | collective-permute-start | bytes 786440 | tf_op jit(solution)/shard_map/ppermute | solution.py:25
  11.6 11.5 %collective-permute-start.1 = (bf16[2,64,1024]{2,1,0:T(8,128)(2,1)S(1)}, bf16[2,64,1024]{2,1,0:T(8,128)(2,1)S(1)}, u32[]{:S(2)}, u32[]{:S(2)}) collective-permute-start(bf16[2,64,1024]{2,1,0:T(8,128)(2,1)S(1)} %collective-permute-done.swapped), channel_id=1, source_target_pairs={{0,32},{1,33},{2,34},{3,35},{4,36},{5,37},{6,38},{7,39},{8,40},{9,... | collective-permute-start | bytes 786440 | tf_op jit(solution)/shard_map/ppermute | solution.py:25
  16.6 6.5 %collective-permute-start.6 = (bf16[2,64,1024]{2,1,0:T(8,128)(2,1)S(1)}, bf16[2,64,1024]{2,1,0:T(8,128)(2,1)S(1)}, u32[]{:S(2)}, u32[]{:S(2)}) collective-permute-start(bf16[2,64,1024]{2,1,0:T(8,128)(2,1)S(1)} %shard_map.30), channel_id=1, source_target_pairs={{0,16},{1,17},{2,18},{3,19},{4,20},{5,21},{6,22},{7,23},{8,24},{9,... | collective-permute-start | bytes 786440 | tf_op jit(solution)/shard_map/ppermute | solution.py:25
  18.6 17.7 %collective-permute-start.15 = (bf16[4,2,64,1024]{3,2,1,0:T(8,128)(2,1)S(1)}, bf16[4,2,64,1024]{3,2,1,0:T(8,128)(2,1)S(1)}, u32[]{:S(2)}, u32[]{:S(2)}) collective-permute-start(bf16[4,2,64,1024]{3,2,1,0:T(8,128)(2,1)S(1)} %shard_map.28.refs_0_.left.ring), channel_id=1, source_target_pairs={{0,3},{1,0},{2,1},{3,2},{4,7},{5,4},{6,5},{7,6},{8,11},{9,8},{10,9... | collective-permute-start | bytes 3145736 | tf_op jit(solution)/shard_map/ppermute | solution.py:25
  20.7 15.6 %collective-permute-start.14 = (bf16[4,2,64,1024]{3,2,1,0:T(8,128)(2,1)S(1)}, bf16[4,2,64,1024]{3,2,1,0:T(8,128)(2,1)S(1)}, u32[]{:S(2)}, u32[]{:S(2)}) collective-permute-start(bf16[4,2,64,1024]{3,2,1,0:T(8,128)(2,1)S(1)} %shard_map.28.refs_0_.left.ring), channel_id=1, source_target_pairs={{0,1},{1,2},{2,3},{3,0},{4,5},{5,6},{6,7},{7,4},{8,9},{9,10},{10,1... | collective-permute-start | bytes 3145736 | tf_op jit(solution)/shard_map/ppermute | solution.py:25
  20.7 5.8 %collective-permute-start.8 = (bf16[2,64,1024]{2,1,0:T(8,128)(2,1)S(1)}, bf16[2,64,1024]{2,1,0:T(8,128)(2,1)S(1)}, u32[]{:S(2)}, u32[]{:S(2)}) collective-permute-start(bf16[2,64,1024]{2,1,0:T(8,128)(2,1)S(1)} %shard_map.30), channel_id=1, source_target_pairs={{0,32},{1,33},{2,34},{3,35},{4,36},{5,37},{6,38},{7,39},{8,40},{9,... | collective-permute-start | bytes 786440 | tf_op jit(solution)/shard_map/ppermute | solution.py:25
  23.7 2.7 %collective-permute-start.9 = (bf16[2,64,1024]{2,1,0:T(8,128)(2,1)S(1)}, bf16[2,64,1024]{2,1,0:T(8,128)(2,1)S(1)}, u32[]{:S(2)}, u32[]{:S(2)}) collective-permute-start(bf16[2,64,1024]{2,1,0:T(8,128)(2,1)S(1)} %shard_map.32), channel_id=1, source_target_pairs={{0,16},{1,17},{2,18},{3,19},{4,20},{5,21},{6,22},{7,23},{8,24},{9,... | collective-permute-start | bytes 786440 | tf_op jit(solution)/shard_map/ppermute | solution.py:25
  23.8 8.0 %collective-permute-start.7 = (bf16[2,64,1024]{2,1,0:T(8,128)(2,1)S(1)}, bf16[2,64,1024]{2,1,0:T(8,128)(2,1)S(1)}, u32[]{:S(2)}, u32[]{:S(2)}) collective-permute-start(bf16[2,64,1024]{2,1,0:T(8,128)(2,1)S(1)} %shard_map.32), channel_id=1, source_target_pairs={{0,32},{1,33},{2,34},{3,35},{4,36},{5,37},{6,38},{7,39},{8,40},{9,... | collective-permute-start | bytes 786440 | tf_op jit(solution)/shard_map/ppermute | solution.py:25
  27.1 4.8 %collective-permute-start.10 = (bf16[2,64,1024]{2,1,0:T(8,128)(2,1)S(1)}, bf16[2,64,1024]{2,1,0:T(8,128)(2,1)S(1)}, u32[]{:S(2)}, u32[]{:S(2)}) collective-permute-start(bf16[2,64,1024]{2,1,0:T(8,128)(2,1)S(1)} %shard_map.34), channel_id=1, source_target_pairs={{0,16},{1,17},{2,18},{3,19},{4,20},{5,21},{6,22},{7,23},{8,24},{9,... | collective-permute-start | bytes 786440 | tf_op jit(solution)/shard_map/ppermute | solution.py:25
  30.1 5.5 %collective-permute-start.12 = (bf16[2,64,1024]{2,1,0:T(8,128)(2,1)S(1)}, bf16[2,64,1024]{2,1,0:T(8,128)(2,1)S(1)}, u32[]{:S(2)}, u32[]{:S(2)}) collective-permute-start(bf16[2,64,1024]{2,1,0:T(8,128)(2,1)S(1)} %shard_map.34), channel_id=1, source_target_pairs={{0,32},{1,33},{2,34},{3,35},{4,36},{5,37},{6,38},{7,39},{8,40},{9,... | collective-permute-start | bytes 786440 | tf_op jit(solution)/shard_map/ppermute | solution.py:25
  32.5 3.1 %collective-permute-start.13 = (bf16[2,64,1024]{2,1,0:T(8,128)(2,1)S(1)}, bf16[2,64,1024]{2,1,0:T(8,128)(2,1)S(1)}, u32[]{:S(2)}, u32[]{:S(2)}) collective-permute-start(bf16[2,64,1024]{2,1,0:T(8,128)(2,1)S(1)} %shard_map.36), channel_id=1, source_target_pairs={{0,16},{1,17},{2,18},{3,19},{4,20},{5,21},{6,22},{7,23},{8,24},{9,... | collective-permute-start | bytes 786440 | tf_op jit(solution)/shard_map/ppermute | solution.py:25
  32.9 6.8 %collective-permute-start.11 = (bf16[2,64,1024]{2,1,0:T(8,128)(2,1)S(1)}, bf16[2,64,1024]{2,1,0:T(8,128)(2,1)S(1)}, u32[]{:S(2)}, u32[]{:S(2)}) collective-permute-start(bf16[2,64,1024]{2,1,0:T(8,128)(2,1)S(1)} %shard_map.36), channel_id=1, source_target_pairs={{0,32},{1,33},{2,34},{3,35},{4,36},{5,37},{6,38},{7,39},{8,40},{9,... | collective-permute-start | bytes 786440 | tf_op jit(solution)/shard_map/ppermute | solution.py:25
  36.3 3.6 %collective-permute-start.16 = (bf16[2,64,1024]{2,1,0:T(8,128)(2,1)S(1)}, bf16[2,64,1024]{2,1,0:T(8,128)(2,1)S(1)}, u32[]{:S(2)}, u32[]{:S(2)}) collective-permute-start(bf16[2,64,1024]{2,1,0:T(8,128)(2,1)S(1)} %shard_map.38), channel_id=1, source_target_pairs={{0,16},{1,17},{2,18},{3,19},{4,20},{5,21},{6,22},{7,23},{8,24},{9,... | collective-permute-start | bytes 786440 | tf_op jit(solution)/shard_map/ppermute | solution.py:25
  40.5 4.2 %collective-permute-start.17 = (bf16[2,64,1024]{2,1,0:T(8,128)(2,1)S(1)}, bf16[2,64,1024]{2,1,0:T(8,128)(2,1)S(1)}, u32[]{:S(2)}, u32[]{:S(2)}) collective-permute-start(bf16[2,64,1024]{2,1,0:T(8,128)(2,1)S(1)} %shard_map.43), channel_id=1, source_target_pairs={{0,16},{1,17},{2,18},{3,19},{4,20},{5,21},{6,22},{7,23},{8,24},{9,... | collective-permute-start | bytes 786440 | tf_op jit(solution)/shard_map/ppermute | solution.py:25
  41.4 11.1 %collective-permute-start.18 = (bf16[2,64,1024]{2,1,0:T(8,128)(2,1)S(1)}, bf16[2,64,1024]{2,1,0:T(8,128)(2,1)S(1)}, u32[]{:S(2)}, u32[]{:S(2)}) collective-permute-start(bf16[2,64,1024]{2,1,0:T(8,128)(2,1)S(1)} %shard_map.38), channel_id=1, source_target_pairs={{0,32},{1,33},{2,34},{3,35},{4,36},{5,37},{6,38},{7,39},{8,40},{9,... | collective-permute-start | bytes 786440 | tf_op jit(solution)/shard_map/ppermute | solution.py:25
  43.0 9.8 %collective-permute-start.21 = (bf16[2,2,64,1024]{3,2,1,0:T(8,128)(2,1)S(1)}, bf16[2,2,64,1024]{3,2,1,0:T(8,128)(2,1)S(1)}, u32[]{:S(2)}, u32[]{:S(2)}) collective-permute-start(bf16[2,2,64,1024]{3,2,1,0:T(8,128)(2,1)S(1)} %slice.9), channel_id=1, source_target_pairs={{0,3},{1,0},{2,1},{3,2},{4,7},{5,4},{6,5},{7,6},{8,11},{9,8},{10,9... | collective-permute-start | bytes 1572872 | tf_op jit(solution)/shard_map/ppermute | solution.py:25
  44.6 9.6 %collective-permute-start.20 = (bf16[2,2,64,1024]{3,2,1,0:T(8,128)(2,1)S(1)}, bf16[2,2,64,1024]{3,2,1,0:T(8,128)(2,1)S(1)}, u32[]{:S(2)}, u32[]{:S(2)}) collective-permute-start(bf16[2,2,64,1024]{3,2,1,0:T(8,128)(2,1)S(1)} %slice.8), channel_id=1, source_target_pairs={{0,1},{1,2},{2,3},{3,0},{4,5},{5,6},{6,7},{7,4},{8,9},{9,10},{10,1... | collective-permute-start | bytes 1572872 | tf_op jit(solution)/shard_map/ppermute | solution.py:25
  52.5 1.7 %collective-permute-start.19 = (bf16[2,64,1024]{2,1,0:T(8,128)(2,1)S(1)}, bf16[2,64,1024]{2,1,0:T(8,128)(2,1)S(1)}, u32[]{:S(2)}, u32[]{:S(2)}) collective-permute-start(bf16[2,64,1024]{2,1,0:T(8,128)(2,1)S(1)} %shard_map.46.far_own), channel_id=1, source_target_pairs={{0,16},{1,17},{2,18},{3,19},{4,20},{5,21},{6,22},{7,23},{8,24},{9,... | collective-permute-start | bytes 786440 | tf_op jit(solution)/shard_map/ppermute | solution.py:25

commit v4 on v3

--- a/solution.py
+++ b/solution.py
@@ -94,27 +94,23 @@
     )(in_hbm(own), *on_chip(*parts))
 
 
-def first_kernel(places, mine, swapped, back, *refs):
-    right, sem = refs[-2:]
-    copy = pltpu.make_async_copy(mine, slot_of(right, places, 0), sem)
-    copy.start()
+def first_kernel(places, swapped, back, *refs):
+    right = refs[-1]
     slot_of(right, places, 1)[...] = swapped[...]
     slot_of(right, places, 2)[...] = back[...]
     for slot in (FAR, FAR + 1):
         slot_of(right, places, slot)[...] = jnp.zeros((2, 64, 1024), jnp.bfloat16)
-    copy.wait()
-
-
-def first(places, mine, swapped, back, *others):
+
+
+def first(places, swapped, back, *others):
     return pl.pallas_call(
         first_kernel,
         out_shape=RIGHT,
-        in_specs=[SMEM, HBM] + [VMEM] * 2 + [ANY] * len(others),
+        in_specs=[SMEM] + [VMEM] * 2 + [ANY] * len(others),
         out_specs=VMEM,
-        scratch_shapes=[pltpu.SemaphoreType.DMA],
         compiler_params=limit(3),
         cost_estimate=cost(0, 2 * MIB),
-    )(places, in_hbm(mine), *on_chip(swapped, back), *others)
+    )(places, *on_chip(swapped, back), *others)
 
 
 def after(values, *others):
@@ -286,15 +282,15 @@
 
     sides = []
     held = [right_panel, swapped]
-    waiting = []
+    waiting = [(0, in_hbm(right_panel))]
     for slot in range(2, FAR, 2):
         step, shard, _ = BLOCKS[slot]
         part = permute(held[shard], along_z(1))
         if slot == 2:
-            right = first(places, right_panel, swapped, part, ring)
+            right = first(places, swapped, part, ring)
         else:
-            due = waiting[:1] if slot < 12 else waiting[:1]
-            waiting = waiting[1:]
+            count = 2 if slot == 4 else 1
+            due, waiting = waiting[:count], waiting[count:]
             right = place(right, [slot] + [s for s, _ in due], [part] + [p for _, p in due], places)
         others = {10: (back, ahead), 12: [s for side in sides for s in side]}.get(slot, ())
         if slot == 10:

time: 60.9 us -> 60.1 us (0.987)
  waiting for transfers between devices: 5.18 us -> 4.06 us
    ppermute x22, waiting for transfers between devices: 5.18 us -> 4.06 us  [permute(): return lax.ppermute(value, AXES, pairs)]
    pallas_call x6, Pallas kernels: 3.66 us -> 4.6 us  [place(): pl.pallas_call(lambda *refs: place_kernel(slots, *refs), out_shape=RIGHT,...]
    pallas_call x1, Pallas kernels: 1.51 us -> 0.62 us  [first(): pl.pallas_call(first_kernel, out_shape=RIGHT, in_specs=[SMEM] + [VMEM] *...]
  transfers between devices with their start and end apart: 22 -> 22, of which waited for: 6 -> 5; matrix products, arithmetic and copies ran while one was open for 0% -> 0% of each run, Pallas kernels for 22% -> 23%
where the time goes in v4:
time: 60.1 us; the launch traced here: 60 us
  starting transfers between devices  34.7 us (58%)
  Pallas kernels  20.8 us (35%)
  waiting for transfers between devices  4.06 us (7%)
    ppermute x22, starting transfers between devices, permute(): return lax.ppermute(value, AXES, pairs)  34.7 us
    pallas_call x1, Pallas kernels, early(): pl.pallas_call(early_kernel, out_shape=pltpu.VMEM((2, 1024, 1024), jnp.fl...  7.14 us
    pallas_call x1, Pallas kernels, late(): pl.pallas_call(late_kernel, grid=(4,), out_shape=jax.ShapeDtypeStruct((2,...  6.49 us
    pallas_call x6, Pallas kernels, place(): pl.pallas_call(lambda *refs: place_kernel(slots, *refs), out_shape=RIGHT,...  4.6 us
    ppermute x22, waiting for transfers between devices, permute(): return lax.ppermute(value, AXES, pairs)  4.06 us
  transfers between devices with their start and end apart: 22, of which 5 were waited for; matrix products, arithmetic and copies ran while one was open for 0% of the time, Pallas kernels for 23%

profile of v4, /device:TPU:1, one launch (start us, length us, event | category | flops | bytes accessed | tf_op | source)
XLA Modules:
  0.0 60.0 jit_solution(16437500963431245727)
XLA Ops:
  0.0 3.2 %collective-permute-start = (bf16[2,64,1024]{2,1,0:T(8,128)(2,1)}, bf16[2,64,1024]{2,1,0:T(8,128)(2,1)S(1)}, u32[]{:S(2)}, u32[]{:S(2)}) collective-permute-start(bf16[2,64,1024]{2,1,0:T(8,128)(2,1)} %refs_2_.1), channel_id=1, source_target_pairs={{0,16},{1,17},{2,18},{3,19},{4,20},{5,21},{6,22},{7,23},{8,24},{9,... | collective-permute-start | bytes 786440 | tf_op jit(solution)/shard_map/ppermute | solution.py:25
  3.2 1.2 %collective-permute-start.5 = (bf16[2,64,1024]{2,1,0:T(8,128)(2,1)}, bf16[2,64,1024]{2,1,0:T(8,128)(2,1)S(1)}, u32[]{:S(2)}, u32[]{:S(2)}) collective-permute-start(bf16[2,64,1024]{2,1,0:T(8,128)(2,1)} %bitcast.17), channel_id=1, source_target_pairs={{0,8},{1,9},{2,10},{3,11},{4,12},{5,13},{6,14},{7,15},{8,0},{9,1},... | collective-permute-start | bytes 786440 | tf_op jit(solution)/shard_map/ppermute | solution.py:25
  4.4 0.8 %collective-permute-start.4 = (bf16[2,64,1024]{2,1,0:T(8,128)(2,1)}, bf16[2,64,1024]{2,1,0:T(8,128)(2,1)S(1)}, u32[]{:S(2)}, u32[]{:S(2)}) collective-permute-start(bf16[2,64,1024]{2,1,0:T(8,128)(2,1)} %bitcast.18), channel_id=1, source_target_pairs={{0,12},{1,13},{2,14},{3,15},{4,0},{5,1},{6,2},{7,3},{8,4},{9,5},{1... | collective-permute-start | bytes 786440 | tf_op jit(solution)/shard_map/ppermute | solution.py:25
  5.2 0.7 %collective-permute-start.3 = (bf16[2,64,1024]{2,1,0:T(8,128)(2,1)}, bf16[2,64,1024]{2,1,0:T(8,128)(2,1)S(1)}, u32[]{:S(2)}, u32[]{:S(2)}) collective-permute-start(bf16[2,64,1024]{2,1,0:T(8,128)(2,1)} %bitcast.19), channel_id=1, source_target_pairs={{0,4},{1,5},{2,6},{3,7},{4,8},{5,9},{6,10},{7,11},{8,12},{9,13},{1... | collective-permute-start | bytes 786440 | tf_op jit(solution)/shard_map/ppermute | solution.py:25
  5.9 5.6 %collective-permute-start.2 = (bf16[2,64,1024]{2,1,0:T(8,128)(2,1)}, bf16[2,64,1024]{2,1,0:T(8,128)(2,1)S(1)}, u32[]{:S(2)}, u32[]{:S(2)}) collective-permute-start(bf16[2,64,1024]{2,1,0:T(8,128)(2,1)} %refs_2_.1), channel_id=1, source_target_pairs={{0,32},{1,33},{2,34},{3,35},{4,36},{5,37},{6,38},{7,39},{8,40},{9,... | collective-permute-start | bytes 786440 | tf_op jit(solution)/shard_map/ppermute | solution.py:25
  11.6 0.8 %collective-permute-start.1 = (bf16[2,64,1024]{2,1,0:T(8,128)(2,1)S(1)}, bf16[2,64,1024]{2,1,0:T(8,128)(2,1)S(1)}, u32[]{:S(2)}, u32[]{:S(2)}) collective-permute-start(bf16[2,64,1024]{2,1,0:T(8,128)(2,1)S(1)} %collective-permute-done.swapped), channel_id=1, source_target_pairs={{0,32},{1,33},{2,34},{3,35},{4,36},{5,37},{6,38},{7,39},{8,40},{9,... | collective-permute-start | bytes 786440 | tf_op jit(solution)/shard_map/ppermute | solution.py:25
  12.4 0.9 %collective-permute-done.3.refs_0_ = bf16[2,64,1024]{2,1,0:T(8,128)(2,1)S(1)} collective-permute-done((bf16[2,64,1024]{2,1,0:T(8,128)(2,1)}, bf16[2,64,1024]{2,1,0:T(8,128)(2,1)S(1)}, u32[]{:S(2)}, u32[]{:S(2)}) %collective-permute-start.3) | collective-permute-done | bytes 262176 | tf_op jit(solution)/shard_map/ppermute | solution.py:25
  13.3 1.0 %shard_map.28.refs_0_.left.ring = bf16[4,2,64,1024]{3,2,1,0:T(8,128)(2,1)S(1)} custom-call(bf16[2,64,1024]{2,1,0:T(8,128)(2,1)} %bitcast.20, bf16[2,64,1024]{2,1,0:T(8,128)(2,1)S(1)} %collective-permute-done.3.refs_0_, bf16[2,64,1024]{2,1,0:T(8,128)(2,1)S(1)} %collective-permute-done.4.refs_1_, bf16[2,64,1024]{2,1,0:T(8,128)(2,1)S(1)} %collective-permute-done.5.refs_2_), custom_call_target="tpu_custom_call" | custom-call | bytes 2097152 | tf_op jit(solution)/shard_map/pallas_call | solution.py:86
  14.2 0.8 %collective-permute-done.2.back.refs_0_ = bf16[2,64,1024]{2,1,0:T(8,128)(2,1)S(1)} collective-permute-done((bf16[2,64,1024]{2,1,0:T(8,128)(2,1)}, bf16[2,64,1024]{2,1,0:T(8,128)(2,1)S(1)}, u32[]{:S(2)}, u32[]{:S(2)}) %collective-permute-start.2) | collective-permute-done | bytes 262176 | tf_op jit(solution)/shard_map/ppermute | solution.py:25
  15.1 0.6 %shard_map.29.refs_1_.refs_4_ = bf16[4,2,4,64,1024]{4,3,2,1,0:T(8,128)(2,1)S(1)} custom-call(s32[16]{0:T(128)S(1)} %fusion.2.places.refs_0_, bf16[2,64,1024]{2,1,0:T(8,128)(2,1)S(1)} %collective-permute-done.swapped, bf16[2,64,1024]{2,1,0:T(8,128)(2,1)S(1)} %collective-permute-done.2.back.refs_0_, bf16[4,2,64,1024]{3,2,1,0:T(8,128)(2,1)S(1)} %shard_map.28.refs_0_.left.ring), custom_call_target="tpu_custom_call" | custom-call | bytes 2097152 | tf_op jit(solution)/shard_map/pallas_call | solution.py:106
  15.7 2.0 %collective-permute-start.6 = (bf16[2,64,1024]{2,1,0:T(8,128)(2,1)S(1)}, bf16[2,64,1024]{2,1,0:T(8,128)(2,1)S(1)}, u32[]{:S(2)}, u32[]{:S(2)}) collective-permute-start(bf16[2,64,1024]{2,1,0:T(8,128)(2,1)S(1)} %shard_map.30), channel_id=1, source_target_pairs={{0,16},{1,17},{2,18},{3,19},{4,20},{5,21},{6,22},{7,23},{8,24},{9,... | collective-permute-start | bytes 786440 | tf_op jit(solution)/shard_map/ppermute | solution.py:25
  17.7 2.1 %collective-permute-start.15 = (bf16[4,2,64,1024]{3,2,1,0:T(8,128)(2,1)S(1)}, bf16[4,2,64,1024]{3,2,1,0:T(8,128)(2,1)S(1)}, u32[]{:S(2)}, u32[]{:S(2)}) collective-permute-start(bf16[4,2,64,1024]{3,2,1,0:T(8,128)(2,1)S(1)} %shard_map.28.refs_0_.left.ring), channel_id=1, source_target_pairs={{0,3},{1,0},{2,1},{3,2},{4,7},{5,4},{6,5},{7,6},{8,11},{9,8},{10,9... | collective-permute-start | bytes 3145736 | tf_op jit(solution)/shard_map/ppermute | solution.py:25
  19.8 2.4 %collective-permute-start.8 = (bf16[2,64,1024]{2,1,0:T(8,128)(2,1)S(1)}, bf16[2,64,1024]{2,1,0:T(8,128)(2,1)S(1)}, u32[]{:S(2)}, u32[]{:S(2)}) collective-permute-start(bf16[2,64,1024]{2,1,0:T(8,128)(2,1)S(1)} %shard_map.30), channel_id=1, source_target_pairs={{0,32},{1,33},{2,34},{3,35},{4,36},{5,37},{6,38},{7,39},{8,40},{9,... | collective-permute-start | bytes 786440 | tf_op jit(solution)/shard_map/ppermute | solution.py:25
  22.2 1.6 %shard_map.31.refs_1_.refs_3_ = bf16[4,2,4,64,1024]{4,3,2,1,0:T(8,128)(2,1)S(1)} custom-call(s32[16]{0:T(128)S(1)} %fusion.2.places.refs_0_, bf16[2,64,1024]{2,1,0:T(8,128)(2,1)S(1)} %collective-permute-done.1.refs_1_.refs_0_, bf16[2,64,1024]{2,1,0:T(8,128)(2,1)} %refs_2_.1, ...), custom_call_target="tpu_custom_call", output_to_operand_aliasing={{}: (4, {})} | custom-call | bytes 524288 | tf_op jit(solution)/shard_map/pallas_call | solution.py:143
  23.9 1.6 %collective-permute-start.7 = (bf16[2,64,1024]{2,1,0:T(8,128)(2,1)S(1)}, bf16[2,64,1024]{2,1,0:T(8,128)(2,1)S(1)}, u32[]{:S(2)}, u32[]{:S(2)}) collective-permute-start(bf16[2,64,1024]{2,1,0:T(8,128)(2,1)S(1)} %shard_map.32), channel_id=1, source_target_pairs={{0,32},{1,33},{2,34},{3,35},{4,36},{5,37},{6,38},{7,39},{8,40},{9,... | collective-permute-start | bytes 786440 | tf_op jit(solution)/shard_map/ppermute | solution.py:25
  25.5 0.6 %shard_map.33.refs_1_.refs_3_ = bf16[4,2,4,64,1024]{4,3,2,1,0:T(8,128)(2,1)S(1)} custom-call(s32[16]{0:T(128)S(1)} %fusion.2.places.refs_0_, bf16[2,64,1024]{2,1,0:T(8,128)(2,1)S(1)} %collective-permute-done.8.refs_1_.refs_0_, bf16[2,64,1024]{2,1,0:T(8,128)(2,1)S(1)} %collective-permute-done.9.refs_2_, ...), custom_call_target="tpu_custom_call", output_to_operand_aliasing={{}: (3, {})} | custom-call | bytes 524288 | tf_op jit(solution)/shard_map/pallas_call | solution.py:143
  26.2 3.0 %collective-permute-start.10 = (bf16[2,64,1024]{2,1,0:T(8,128)(2,1)S(1)}, bf16[2,64,1024]{2,1,0:T(8,128)(2,1)S(1)}, u32[]{:S(2)}, u32[]{:S(2)}) collective-permute-start(bf16[2,64,1024]{2,1,0:T(8,128)(2,1)S(1)} %shard_map.34), channel_id=1, source_target_pairs={{0,16},{1,17},{2,18},{3,19},{4,20},{5,21},{6,22},{7,23},{8,24},{9,... | collective-permute-start | bytes 786440 | tf_op jit(solution)/shard_map/ppermute | solution.py:25
  29.2 1.7 %collective-permute-start.12 = (bf16[2,64,1024]{2,1,0:T(8,128)(2,1)S(1)}, bf16[2,64,1024]{2,1,0:T(8,128)(2,1)S(1)}, u32[]{:S(2)}, u32[]{:S(2)}) collective-permute-start(bf16[2,64,1024]{2,1,0:T(8,128)(2,1)S(1)} %shard_map.34), channel_id=1, source_target_pairs={{0,32},{1,33},{2,34},{3,35},{4,36},{5,37},{6,38},{7,39},{8,40},{9,... | collective-permute-start | bytes 786440 | tf_op jit(solution)/shard_map/ppermute | solution.py:25
  31.0 0.6 %shard_map.35.refs_1_.refs_3_ = bf16[4,2,4,64,1024]{4,3,2,1,0:T(8,128)(2,1)S(1)} custom-call(s32[16]{0:T(128)S(1)} %fusion.2.places.refs_0_, bf16[2,64,1024]{2,1,0:T(8,128)(2,1)S(1)} %collective-permute-done.7.refs_1_.refs_0_, bf16[2,64,1024]{2,1,0:T(8,128)(2,1)S(1)} %collective-permute-done.10.refs_2_, ...), custom_call_target="tpu_custom_call", output_to_operand_aliasing={{}: (3, {})} | custom-call | bytes 524288 | tf_op jit(solution)/shard_map/pallas_call | solution.py:143
  31.6 1.1 %collective-permute-start.13 = (bf16[2,64,1024]{2,1,0:T(8,128)(2,1)S(1)}, bf16[2,64,1024]{2,1,0:T(8,128)(2,1)S(1)}, u32[]{:S(2)}, u32[]{:S(2)}) collective-permute-start(bf16[2,64,1024]{2,1,0:T(8,128)(2,1)S(1)} %shard_map.36), channel_id=1, source_target_pairs={{0,16},{1,17},{2,18},{3,19},{4,20},{5,21},{6,22},{7,23},{8,24},{9,... | collective-permute-start | bytes 786440 | tf_op jit(solution)/shard_map/ppermute | solution.py:25
  32.7 1.1 %collective-permute-start.11 = (bf16[2,64,1024]{2,1,0:T(8,128)(2,1)S(1)}, bf16[2,64,1024]{2,1,0:T(8,128)(2,1)S(1)}, u32[]{:S(2)}, u32[]{:S(2)}) collective-permute-start(bf16[2,64,1024]{2,1,0:T(8,128)(2,1)S(1)} %shard_map.36), channel_id=1, source_target_pairs={{0,32},{1,33},{2,34},{3,35},{4,36},{5,37},{6,38},{7,39},{8,40},{9,... | collective-permute-start | bytes 786440 | tf_op jit(solution)/shard_map/ppermute | solution.py:25
  33.8 1.0 %collective-permute-done.12.refs_1_.refs_0_ = bf16[2,64,1024]{2,1,0:T(8,128)(2,1)S(1)} collective-permute-done((bf16[2,64,1024]{2,1,0:T(8,128)(2,1)S(1)}, bf16[2,64,1024]{2,1,0:T(8,128)(2,1)S(1)}, u32[]{:S(2)}, u32[]{:S(2)}) %collective-permute-start.12) | collective-permute-done | bytes 262176 | tf_op jit(solution)/shard_map/ppermute | solution.py:25
  34.7 0.6 %shard_map.37.refs_1_.refs_3_ = bf16[4,2,4,64,1024]{4,3,2,1,0:T(8,128)(2,1)S(1)} custom-call(s32[16]{0:T(128)S(1)} %fusion.2.places.refs_0_, bf16[2,64,1024]{2,1,0:T(8,128)(2,1)S(1)} %collective-permute-done.12.refs_1_.refs_0_, bf16[2,64,1024]{2,1,0:T(8,128)(2,1)S(1)} %collective-permute-done.13.refs_2_, ...), custom_call_target="tpu_custom_call", output_to_operand_aliasing={{}: (3, {})} | custom-call | bytes 524288 | tf_op jit(solution)/shard_map/pallas_call | solution.py:143
  35.4 2.4 %collective-permute-start.16 = (bf16[2,64,1024]{2,1,0:T(8,128)(2,1)S(1)}, bf16[2,64,1024]{2,1,0:T(8,128)(2,1)S(1)}, u32[]{:S(2)}, u32[]{:S(2)}) collective-permute-start(bf16[2,64,1024]{2,1,0:T(8,128)(2,1)S(1)} %shard_map.38), channel_id=1, source_target_pairs={{0,16},{1,17},{2,18},{3,19},{4,20},{5,21},{6,22},{7,23},{8,24},{9,... | collective-permute-start | bytes 786440 | tf_op jit(solution)/shard_map/ppermute | solution.py:25
  39.0 0.6 %shard_map.39.refs_1_.refs_2_ = bf16[4,2,4,64,1024]{4,3,2,1,0:T(8,128)(2,1)S(1)} custom-call(s32[16]{0:T(128)S(1)} %fusion.2.places.refs_0_, bf16[2,64,1024]{2,1,0:T(8,128)(2,1)S(1)} %collective-permute-done.11.refs_1_.refs_0_, bf16[2,64,1024]{2,1,0:T(8,128)(2,1)S(1)} %collective-permute-done.16.refs_2_, ...), custom_call_target="tpu_custom_call", output_to_operand_aliasing={{}: (3, {})} | custom-call | bytes 524288 | tf_op jit(solution)/shard_map/pallas_call | solution.py:143
  39.6 1.5 %collective-permute-start.17 = (bf16[2,64,1024]{2,1,0:T(8,128)(2,1)S(1)}, bf16[2,64,1024]{2,1,0:T(8,128)(2,1)S(1)}, u32[]{:S(2)}, u32[]{:S(2)}) collective-permute-start(bf16[2,64,1024]{2,1,0:T(8,128)(2,1)S(1)} %shard_map.43), channel_id=1, source_target_pairs={{0,16},{1,17},{2,18},{3,19},{4,20},{5,21},{6,22},{7,23},{8,24},{9,... | collective-permute-start | bytes 786440 | tf_op jit(solution)/shard_map/ppermute | solution.py:25
  41.1 1.0 %collective-permute-start.18 = (bf16[2,64,1024]{2,1,0:T(8,128)(2,1)S(1)}, bf16[2,64,1024]{2,1,0:T(8,128)(2,1)S(1)}, u32[]{:S(2)}, u32[]{:S(2)}) collective-permute-start(bf16[2,64,1024]{2,1,0:T(8,128)(2,1)S(1)} %shard_map.38), channel_id=1, source_target_pairs={{0,32},{1,33},{2,34},{3,35},{4,36},{5,37},{6,38},{7,39},{8,40},{9,... | collective-permute-start | bytes 786440 | tf_op jit(solution)/shard_map/ppermute | solution.py:25
  42.2 1.7 %collective-permute-start.21 = (bf16[2,2,64,1024]{3,2,1,0:T(8,128)(2,1)S(1)}, bf16[2,2,64,1024]{3,2,1,0:T(8,128)(2,1)S(1)}, u32[]{:S(2)}, u32[]{:S(2)}) collective-permute-start(bf16[2,2,64,1024]{3,2,1,0:T(8,128)(2,1)S(1)} %slice.9), channel_id=1, source_target_pairs={{0,3},{1,0},{2,1},{3,2},{4,7},{5,4},{6,5},{7,6},{8,11},{9,8},{10,9... | collective-permute-start | bytes 1572872 | tf_op jit(solution)/shard_map/ppermute | solution.py:25
  44.0 0.6 shard_map.44.right
  44.6 7.1 %shard_map.45.refs_1_.acc = f32[2,1024,1024]{2,1,0:T(8,128)S(1)} custom-call(bf16[4,2,4,64,1024]{4,3,2,1,0:T(8,128)(2,1)S(1)} %shard_map.44.right, bf16[1024,512]{1,0:T(8,128)(2,1)S(1)} %get-tuple-element.11.refs_2_.refs_0_, bf16[1024,512]{1,0:T(8,128)(2,1)S(1)} %get-tuple-element.12.refs_3_.refs_1_, ...), custom_call_target="tpu_custom_call" | custom-call | flops 6442450944 | bytes 8388608 | tf_op jit(solution)/shard_map/pallas_call | solution.py:194
  52.3 1.2 %collective-permute-done.20.up = bf16[2,2,64,1024]{3,2,1,0:T(8,128)(2,1)S(1)} collective-permute-done((bf16[2,2,64,1024]{3,2,1,0:T(8,128)(2,1)S(1)}, bf16[2,2,64,1024]{3,2,1,0:T(8,128)(2,1)S(1)}, u32[]{:S(2)}, u32[]{:S(2)}) %collective-permute-start.20) | collective-permute-done | bytes 524320 | tf_op jit(solution)/shard_map/ppermute | solution.py:25
  53.5 6.5 %shard_map.47 = f32[2,1024,1024]{2,1,0:T(8,128)} custom-call(s32[16]{0:T(128)S(1)} %fusion.2.places.refs_0_, f32[2,1024,1024]{2,1,0:T(8,128)S(1)} %shard_map.45.refs_1_.acc, bf16[4,2,4,64,1024]{4,3,2,1,0:T(8,128)(2,1)S(1)} %shard_map.44.right, bf16[2,64,1024]{2,1,0:T(8,128)(2,1)S(1)} %shard_map.46.far_own, ...), custom_call_target="tpu_custom_call" | custom-call | flops 3221225472 | bytes 9437184 | tf_op jit(solution)/shard_map/pallas_call | solution.py:237
  (36 shorter events, 2.1 us)
Async XLA Ops:
  0.0 11.6 %collective-permute-start = (bf16[2,64,1024]{2,1,0:T(8,128)(2,1)}, bf16[2,64,1024]{2,1,0:T(8,128)(2,1)S(1)}, u32[]{:S(2)}, u32[]{:S(2)}) collective-permute-start(bf16[2,64,1024]{2,1,0:T(8,128)(2,1)} %refs_2_.1), channel_id=1, source_target_pairs={{0,16},{1,17},{2,18},{3,19},{4,20},{5,21},{6,22},{7,23},{8,24},{9,... | collective-permute-start | bytes 786440 | tf_op jit(solution)/shard_map/ppermute | solution.py:25
  3.2 9.2 %collective-permute-start.5 = (bf16[2,64,1024]{2,1,0:T(8,128)(2,1)}, bf16[2,64,1024]{2,1,0:T(8,128)(2,1)S(1)}, u32[]{:S(2)}, u32[]{:S(2)}) collective-permute-start(bf16[2,64,1024]{2,1,0:T(8,128)(2,1)} %bitcast.17), channel_id=1, source_target_pairs={{0,8},{1,9},{2,10},{3,11},{4,12},{5,13},{6,14},{7,15},{8,0},{9,1},... | collective-permute-start | bytes 786440 | tf_op jit(solution)/shard_map/ppermute | solution.py:25
  4.4 8.0 %collective-permute-start.4 = (bf16[2,64,1024]{2,1,0:T(8,128)(2,1)}, bf16[2,64,1024]{2,1,0:T(8,128)(2,1)S(1)}, u32[]{:S(2)}, u32[]{:S(2)}) collective-permute-start(bf16[2,64,1024]{2,1,0:T(8,128)(2,1)} %bitcast.18), channel_id=1, source_target_pairs={{0,12},{1,13},{2,14},{3,15},{4,0},{5,1},{6,2},{7,3},{8,4},{9,5},{1... | collective-permute-start | bytes 786440 | tf_op jit(solution)/shard_map/ppermute | solution.py:25
  5.2 8.1 %collective-permute-start.3 = (bf16[2,64,1024]{2,1,0:T(8,128)(2,1)}, bf16[2,64,1024]{2,1,0:T(8,128)(2,1)S(1)}, u32[]{:S(2)}, u32[]{:S(2)}) collective-permute-start(bf16[2,64,1024]{2,1,0:T(8,128)(2,1)} %bitcast.19), channel_id=1, source_target_pairs={{0,4},{1,5},{2,6},{3,7},{4,8},{5,9},{6,10},{7,11},{8,12},{9,13},{1... | collective-permute-start | bytes 786440 | tf_op jit(solution)/shard_map/ppermute | solution.py:25
  5.9 9.2 %collective-permute-start.2 = (bf16[2,64,1024]{2,1,0:T(8,128)(2,1)}, bf16[2,64,1024]{2,1,0:T(8,128)(2,1)S(1)}, u32[]{:S(2)}, u32[]{:S(2)}) collective-permute-start(bf16[2,64,1024]{2,1,0:T(8,128)(2,1)} %refs_2_.1), channel_id=1, source_target_pairs={{0,32},{1,33},{2,34},{3,35},{4,36},{5,37},{6,38},{7,39},{8,40},{9,... | collective-permute-start | bytes 786440 | tf_op jit(solution)/shard_map/ppermute | solution.py:25
  11.6 10.6 %collective-permute-start.1 = (bf16[2,64,1024]{2,1,0:T(8,128)(2,1)S(1)}, bf16[2,64,1024]{2,1,0:T(8,128)(2,1)S(1)}, u32[]{:S(2)}, u32[]{:S(2)}) collective-permute-start(bf16[2,64,1024]{2,1,0:T(8,128)(2,1)S(1)} %collective-permute-done.swapped), channel_id=1, source_target_pairs={{0,32},{1,33},{2,34},{3,35},{4,36},{5,37},{6,38},{7,39},{8,40},{9,... | collective-permute-start | bytes 786440 | tf_op jit(solution)/shard_map/ppermute | solution.py:25
  15.7 6.5 %collective-permute-start.6 = (bf16[2,64,1024]{2,1,0:T(8,128)(2,1)S(1)}, bf16[2,64,1024]{2,1,0:T(8,128)(2,1)S(1)}, u32[]{:S(2)}, u32[]{:S(2)}) collective-permute-start(bf16[2,64,1024]{2,1,0:T(8,128)(2,1)S(1)} %shard_map.30), channel_id=1, source_target_pairs={{0,16},{1,17},{2,18},{3,19},{4,20},{5,21},{6,22},{7,23},{8,24},{9,... | collective-permute-start | bytes 786440 | tf_op jit(solution)/shard_map/ppermute | solution.py:25
  17.7 17.7 %collective-permute-start.15 = (bf16[4,2,64,1024]{3,2,1,0:T(8,128)(2,1)S(1)}, bf16[4,2,64,1024]{3,2,1,0:T(8,128)(2,1)S(1)}, u32[]{:S(2)}, u32[]{:S(2)}) collective-permute-start(bf16[4,2,64,1024]{3,2,1,0:T(8,128)(2,1)S(1)} %shard_map.28.refs_0_.left.ring), channel_id=1, source_target_pairs={{0,3},{1,0},{2,1},{3,2},{4,7},{5,4},{6,5},{7,6},{8,11},{9,8},{10,9... | collective-permute-start | bytes 3145736 | tf_op jit(solution)/shard_map/ppermute | solution.py:25
  19.8 15.6 %collective-permute-start.14 = (bf16[4,2,64,1024]{3,2,1,0:T(8,128)(2,1)S(1)}, bf16[4,2,64,1024]{3,2,1,0:T(8,128)(2,1)S(1)}, u32[]{:S(2)}, u32[]{:S(2)}) collective-permute-start(bf16[4,2,64,1024]{3,2,1,0:T(8,128)(2,1)S(1)} %shard_map.28.refs_0_.left.ring), channel_id=1, source_target_pairs={{0,1},{1,2},{2,3},{3,0},{4,5},{5,6},{6,7},{7,4},{8,9},{9,10},{10,1... | collective-permute-start | bytes 3145736 | tf_op jit(solution)/shard_map/ppermute | solution.py:25
  19.8 5.8 %collective-permute-start.8 = (bf16[2,64,1024]{2,1,0:T(8,128)(2,1)S(1)}, bf16[2,64,1024]{2,1,0:T(8,128)(2,1)S(1)}, u32[]{:S(2)}, u32[]{:S(2)}) collective-permute-start(bf16[2,64,1024]{2,1,0:T(8,128)(2,1)S(1)} %shard_map.30), channel_id=1, source_target_pairs={{0,32},{1,33},{2,34},{3,35},{4,36},{5,37},{6,38},{7,39},{8,40},{9,... | collective-permute-start | bytes 786440 | tf_op jit(solution)/shard_map/ppermute | solution.py:25
  23.8 1.7 %collective-permute-start.9 = (bf16[2,64,1024]{2,1,0:T(8,128)(2,1)S(1)}, bf16[2,64,1024]{2,1,0:T(8,128)(2,1)S(1)}, u32[]{:S(2)}, u32[]{:S(2)}) collective-permute-start(bf16[2,64,1024]{2,1,0:T(8,128)(2,1)S(1)} %shard_map.32), channel_id=1, source_target_pairs={{0,16},{1,17},{2,18},{3,19},{4,20},{5,21},{6,22},{7,23},{8,24},{9,... | collective-permute-start | bytes 786440 | tf_op jit(solution)/shard_map/ppermute | solution.py:25
  23.9 7.1 %collective-permute-start.7 = (bf16[2,64,1024]{2,1,0:T(8,128)(2,1)S(1)}, bf16[2,64,1024]{2,1,0:T(8,128)(2,1)S(1)}, u32[]{:S(2)}, u32[]{:S(2)}) collective-permute-start(bf16[2,64,1024]{2,1,0:T(8,128)(2,1)S(1)} %shard_map.32), channel_id=1, source_target_pairs={{0,32},{1,33},{2,34},{3,35},{4,36},{5,37},{6,38},{7,39},{8,40},{9,... | collective-permute-start | bytes 786440 | tf_op jit(solution)/shard_map/ppermute | solution.py:25
  26.2 4.8 %collective-permute-start.10 = (bf16[2,64,1024]{2,1,0:T(8,128)(2,1)S(1)}, bf16[2,64,1024]{2,1,0:T(8,128)(2,1)S(1)}, u32[]{:S(2)}, u32[]{:S(2)}) collective-permute-start(bf16[2,64,1024]{2,1,0:T(8,128)(2,1)S(1)} %shard_map.34), channel_id=1, source_target_pairs={{0,16},{1,17},{2,18},{3,19},{4,20},{5,21},{6,22},{7,23},{8,24},{9,... | collective-permute-start | bytes 786440 | tf_op jit(solution)/shard_map/ppermute | solution.py:25
  29.2 5.5 %collective-permute-start.12 = (bf16[2,64,1024]{2,1,0:T(8,128)(2,1)S(1)}, bf16[2,64,1024]{2,1,0:T(8,128)(2,1)S(1)}, u32[]{:S(2)}, u32[]{:S(2)}) collective-permute-start(bf16[2,64,1024]{2,1,0:T(8,128)(2,1)S(1)} %shard_map.34), channel_id=1, source_target_pairs={{0,32},{1,33},{2,34},{3,35},{4,36},{5,37},{6,38},{7,39},{8,40},{9,... | collective-permute-start | bytes 786440 | tf_op jit(solution)/shard_map/ppermute | solution.py:25
  31.6 3.1 %collective-permute-start.13 = (bf16[2,64,1024]{2,1,0:T(8,128)(2,1)S(1)}, bf16[2,64,1024]{2,1,0:T(8,128)(2,1)S(1)}, u32[]{:S(2)}, u32[]{:S(2)}) collective-permute-start(bf16[2,64,1024]{2,1,0:T(8,128)(2,1)S(1)} %shard_map.36), channel_id=1, source_target_pairs={{0,16},{1,17},{2,18},{3,19},{4,20},{5,21},{6,22},{7,23},{8,24},{9,... | collective-permute-start | bytes 786440 | tf_op jit(solution)/shard_map/ppermute | solution.py:25
  32.7 6.1 %collective-permute-start.11 = (bf16[2,64,1024]{2,1,0:T(8,128)(2,1)S(1)}, bf16[2,64,1024]{2,1,0:T(8,128)(2,1)S(1)}, u32[]{:S(2)}, u32[]{:S(2)}) collective-permute-start(bf16[2,64,1024]{2,1,0:T(8,128)(2,1)S(1)} %shard_map.36), channel_id=1, source_target_pairs={{0,32},{1,33},{2,34},{3,35},{4,36},{5,37},{6,38},{7,39},{8,40},{9,... | collective-permute-start | bytes 786440 | tf_op jit(solution)/shard_map/ppermute | solution.py:25
  35.4 3.6 %collective-permute-start.16 = (bf16[2,64,1024]{2,1,0:T(8,128)(2,1)S(1)}, bf16[2,64,1024]{2,1,0:T(8,128)(2,1)S(1)}, u32[]{:S(2)}, u32[]{:S(2)}) collective-permute-start(bf16[2,64,1024]{2,1,0:T(8,128)(2,1)S(1)} %shard_map.38), channel_id=1, source_target_pairs={{0,16},{1,17},{2,18},{3,19},{4,20},{5,21},{6,22},{7,23},{8,24},{9,... | collective-permute-start | bytes 786440 | tf_op jit(solution)/shard_map/ppermute | solution.py:25
  39.6 4.4 %collective-permute-start.17 = (bf16[2,64,1024]{2,1,0:T(8,128)(2,1)S(1)}, bf16[2,64,1024]{2,1,0:T(8,128)(2,1)S(1)}, u32[]{:S(2)}, u32[]{:S(2)}) collective-permute-start(bf16[2,64,1024]{2,1,0:T(8,128)(2,1)S(1)} %shard_map.43), channel_id=1, source_target_pairs={{0,16},{1,17},{2,18},{3,19},{4,20},{5,21},{6,22},{7,23},{8,24},{9,... | collective-permute-start | bytes 786440 | tf_op jit(solution)/shard_map/ppermute | solution.py:25
  41.1 10.6 %collective-permute-start.18 = (bf16[2,64,1024]{2,1,0:T(8,128)(2,1)S(1)}, bf16[2,64,1024]{2,1,0:T(8,128)(2,1)S(1)}, u32[]{:S(2)}, u32[]{:S(2)}) collective-permute-start(bf16[2,64,1024]{2,1,0:T(8,128)(2,1)S(1)} %shard_map.38), channel_id=1, source_target_pairs={{0,32},{1,33},{2,34},{3,35},{4,36},{5,37},{6,38},{7,39},{8,40},{9,... | collective-permute-start | bytes 786440 | tf_op jit(solution)/shard_map/ppermute | solution.py:25
  42.2 10.2 %collective-permute-start.21 = (bf16[2,2,64,1024]{3,2,1,0:T(8,128)(2,1)S(1)}, bf16[2,2,64,1024]{3,2,1,0:T(8,128)(2,1)S(1)}, u32[]{:S(2)}, u32[]{:S(2)}) collective-permute-start(bf16[2,2,64,1024]{3,2,1,0:T(8,128)(2,1)S(1)} %slice.9), channel_id=1, source_target_pairs={{0,3},{1,0},{2,1},{3,2},{4,7},{5,4},{6,5},{7,6},{8,11},{9,8},{10,9... | collective-permute-start | bytes 1572872 | tf_op jit(solution)/shard_map/ppermute | solution.py:25
  43.9 9.6 %collective-permute-start.20 = (bf16[2,2,64,1024]{3,2,1,0:T(8,128)(2,1)S(1)}, bf16[2,2,64,1024]{3,2,1,0:T(8,128)(2,1)S(1)}, u32[]{:S(2)}, u32[]{:S(2)}) collective-permute-start(bf16[2,2,64,1024]{3,2,1,0:T(8,128)(2,1)S(1)} %slice.8), channel_id=1, source_target_pairs={{0,1},{1,2},{2,3},{3,0},{4,5},{5,6},{6,7},{7,4},{8,9},{9,10},{10,1... | collective-permute-start | bytes 1572872 | tf_op jit(solution)/shard_map/ppermute | solution.py:25
  51.8 1.8 %collective-permute-start.19 = (bf16[2,64,1024]{2,1,0:T(8,128)(2,1)S(1)}, bf16[2,64,1024]{2,1,0:T(8,128)(2,1)S(1)}, u32[]{:S(2)}, u32[]{:S(2)}) collective-permute-start(bf16[2,64,1024]{2,1,0:T(8,128)(2,1)S(1)} %shard_map.46.far_own), channel_id=1, source_target_pairs={{0,16},{1,17},{2,18},{3,19},{4,20},{5,21},{6,22},{7,23},{8,24},{9,... | collective-permute-start | bytes 786440 | tf_op jit(solution)/shard_map/ppermute | solution.py:25
